TPU v7x, 512 devices: a whole 4x8x8 slice. The times are simulated.
512 devices in a mesh: gx: 32 (over y, x), yz: 16 (over z, core).
Axes of the slice: x: 4, y: 8, z: 8, core: 2. Of those that a mesh axis runs over, the one named last changes fastest.
Arguments:
- thermal_state_initial: float32 [1024, 1024, 128], P('gx', 'yz'), may hold values from -5 to 5
- x_conductance_scaled: float32 [1024, 1024, 128], P('gx', 'yz'), may hold values from 30000 to 100000
- y_conductance_scaled: float32 [1024, 128], P('yz'), may hold values from 0.05 to 0.4
- z_conductance_scaled: float32 [1024, 128], P('yz'), may hold values from 0.05 to 0.4
Outputs:
- updated: float32 [1024, 1024, 128], P('gx', 'yz')
All inputs are finite; a program needn't handle non-finite values.
Results may differ from a plain program's by a relative error of at most 0.00055.
Values sent between devices are 32-bit elements; how exact they have to be, the bound alone decides.
A program may use at most 64 MiB of HBM per device.

v0:
```python
import jax
import jax.numpy as jnp
from jax import lax
from jax.sharding import PartitionSpec as P


def with_halo(cells, sides, width):
    for axis, dim in sides:
        count = lax.axis_size(axis)
        ends = count - 1
        head = lax.slice_in_dim(cells, 0, width, axis=dim)
        tail = lax.slice_in_dim(cells, cells.shape[dim] - width, cells.shape[dim], axis=dim)
        cells = jnp.concatenate(
            [
                lax.ppermute(tail, axis, [(i, (i + 1) % count) for i in range(ends)]),
                cells,
                lax.ppermute(head, axis, [((i + 1) % count, i) for i in range(ends)]),
            ],
            axis=dim,
        )
    return cells


def shifted(block, axis, distance):
    devices = range(lax.axis_size(axis))
    route = [(i - distance, i) for i in devices if i - distance in devices]
    return lax.ppermute(block, axis, route)


def reduce_level(current, from_lower, from_upper, lower_valid, upper_valid):
    ratio_lower = jnp.where(
        lower_valid, current[0] / jnp.where(lower_valid, from_lower[1], 1.0), 0.0
    )
    ratio_upper = jnp.where(
        upper_valid, current[2] / jnp.where(upper_valid, from_upper[1], 1.0), 0.0
    )
    new_first = -ratio_lower * from_lower[0]
    new_third = -ratio_upper * from_upper[2]
    new_second = current[1] - ratio_lower * from_lower[2] - ratio_upper * from_upper[0]
    new_fourth = current[3] - ratio_lower * from_lower[3] - ratio_upper * from_upper[3]
    return (new_first, new_second, new_third, new_fourth)


def shards(thermal_state_initial, x_conductance_scaled, y_conductance_scaled, z_conductance_scaled):
    volumes_along_x, volumes_along_y, volumes_along_z = thermal_state_initial.shape
    bordered_field_values = with_halo(thermal_state_initial, (("gx", 0), ("yz", 1)), 1)
    next_x = shifted(x_conductance_scaled[:1], "gx", -1)
    next_y = shifted(y_conductance_scaled[:1], "yz", -1)
    x_coupling_higher = jnp.concatenate([x_conductance_scaled[1:], next_x], 0)
    y_coupling_higher = jnp.concatenate([y_conductance_scaled[1:], next_y], 0)
    z_coupling_higher = jnp.concatenate(
        [z_conductance_scaled[:, 1:], jnp.zeros((volumes_along_y, 1), jnp.float32)], 1
    )
    vacant_slab = jnp.zeros((volumes_along_x, volumes_along_y, 1), jnp.float32)
    z_adjacent_smaller = jnp.concatenate([vacant_slab, thermal_state_initial[:, :, :-1]], 2)
    z_adjacent_higher = jnp.concatenate([thermal_state_initial[:, :, 1:], vacant_slab], 2)
    thermal_current_x = x_conductance_scaled * (
        thermal_state_initial - bordered_field_values[:-2, 1:-1]
    ) + x_coupling_higher * (thermal_state_initial - bordered_field_values[2:, 1:-1])
    thermal_current_y = y_conductance_scaled[None] * (
        thermal_state_initial - bordered_field_values[1:-1, :-2]
    ) + y_coupling_higher[None] * (thermal_state_initial - bordered_field_values[1:-1, 2:])
    thermal_current_z = z_conductance_scaled[None] * (
        thermal_state_initial - z_adjacent_smaller
    ) + z_coupling_higher[None] * (thermal_state_initial - z_adjacent_higher)
    forcing_contribution = (
        thermal_state_initial - 0.5 * thermal_current_x - thermal_current_y - thermal_current_z
    )
    lower_coef = 0.5 * x_conductance_scaled
    upper_coef = 0.5 * x_coupling_higher
    diagonal = 1.0 + lower_coef + upper_coef
    inner_count = volumes_along_x - 1
    blank_plane = jnp.zeros((volumes_along_y, volumes_along_z), jnp.float32)
    factor_prev = blank_plane
    partial_prev = jnp.zeros((3, volumes_along_y, volumes_along_z), jnp.float32)
    factors = []
    partials = []
    for stripe_position_id in range(inner_count):
        divisor = diagonal[stripe_position_id] - lower_coef[stripe_position_id] * factor_prev
        factor_prev = upper_coef[stripe_position_id] / divisor
        start_term = lower_coef[0] if stripe_position_id == 0 else blank_plane
        end_term = (
            upper_coef[inner_count - 1] if stripe_position_id == inner_count - 1 else blank_plane
        )
        stacked = jnp.stack([forcing_contribution[stripe_position_id], start_term, end_term])
        partial_prev = (stacked + lower_coef[stripe_position_id] * partial_prev) / divisor
        factors.append(factor_prev)
        partials.append(partial_prev)
    eliminated = [None] * inner_count
    solution_row = partials[inner_count - 1]
    eliminated[inner_count - 1] = solution_row
    for stripe_position_id in range(inner_count - 2, -1, -1):
        solution_row = partials[stripe_position_id] + factors[stripe_position_id] * solution_row
        eliminated[stripe_position_id] = solution_row
    inner_last = eliminated[inner_count - 1]
    next_first = shifted(eliminated[0], "gx", -1)
    lower_last = lower_coef[volumes_along_x - 1]
    upper_last = upper_coef[volumes_along_x - 1]
    system = (
        -lower_last * inner_last[1],
        diagonal[volumes_along_x - 1] - lower_last * inner_last[2] - upper_last * next_first[1],
        -upper_last * next_first[2],
        forcing_contribution[volumes_along_x - 1]
        + lower_last * inner_last[0]
        + upper_last * next_first[0],
    )
    position = lax.axis_index("gx")
    group_size = lax.axis_size("gx")
    distance = 1
    while distance < group_size:
        packed = jnp.stack(system)
        from_lower = shifted(packed, "gx", distance)
        from_upper = shifted(packed, "gx", -distance)
        system = reduce_level(
            system,
            tuple(from_lower),
            tuple(from_upper),
            position >= distance,
            position + distance < group_size,
        )
        distance = distance * 2
    interface = system[3] / system[1]
    previous = shifted(interface, "gx", 1)
    inner_stack = jnp.stack(eliminated)
    inner_rows = (
        inner_stack[:, 0] + inner_stack[:, 1] * previous[None] + inner_stack[:, 2] * interface[None]
    )
    return jnp.concatenate([inner_rows, interface[None]], 0)


def solution(mesh):
    return jax.shard_map(
        shards,
        mesh=mesh,
        in_specs=(P("gx", "yz", None), P("gx", "yz", None), P("yz", None), P("yz", None)),
        out_specs=P("gx", "yz", None),
        check_vma=False,
    )
```

profile of v0, /device:TPU:200, one launch (start us, length us, event | category | flops | bytes accessed | tf_op | source)
XLA Modules:
  0.0 113.7 jit_solution(4308513147861316245)
XLA Ops:
  0.9 3.4 %collective-permute-start = (f32[1,64,128]{2,1,0:T(8,128)S(1)}, f32[1,64,128]{2,1,0:T(8,128)S(1)}, u32[]{:S(2)}, u32[]{:S(2)}) collective-permute-start(f32[1,64,128]{2,1,0:T(8,128)S(1)} %get-tuple-element.188), channel_id=1, source_target_pairs={{0,16},{16,32},{32,48},{48,64},{64,80},{80,96},{96,112},{112,128},... | collective-permute-start | bytes 98312 | tf_op jit(solution)/shard_map/ppermute | solution.py:15
  4.3 4.6 %collective-permute-start.2 = (f32[1,64,128]{2,1,0:T(8,128)S(1)}, f32[1,64,128]{2,1,0:T(8,128)S(1)}, u32[]{:S(2)}, u32[]{:S(2)}) collective-permute-start(f32[1,64,128]{2,1,0:T(8,128)S(1)} %get-tuple-element.187), channel_id=1, source_target_pairs={{16,0},{32,16},{48,32},{64,48},{80,64},{96,80},{112,96},{128,112},... | collective-permute-start | bytes 98312 | tf_op jit(solution)/shard_map/ppermute | solution.py:17
  9.6 2.4 %collective-permute-start.1 = (f32[1,64,128]{2,1,0:T(8,128)S(1)}, f32[1,64,128]{2,1,0:T(8,128)S(1)}, u32[]{:S(2)}, u32[]{:S(2)}) collective-permute-start(f32[1,64,128]{2,1,0:T(8,128)S(1)} %slice.495), channel_id=1, source_target_pairs={{16,0},{32,16},{48,32},{64,48},{80,64},{96,80},{112,96},{128,112},... | collective-permute-start | bytes 98312 | tf_op jit(solution)/shard_map/ppermute | solution.py:27
  12.7 2.0 %collective-permute-start.4 = (f32[1,128]{1,0:T(1,128)S(1)}, f32[1,128]{1,0:T(1,128)S(1)}, u32[]{:S(2)}, u32[]{:S(2)}) collective-permute-start(f32[1,128]{1,0:T(1,128)S(1)} %slice.501), channel_id=1, source_target_pairs={{1,0},{2,1},{3,2},{4,3},{5,4},{6,5},{7,6},{8,7},{9,8},{10,9},{11,1... | collective-permute-start | bytes 1544 | tf_op jit(solution)/shard_map/ppermute | solution.py:27
  14.8 3.4 %fusion.108 = (f32[32,64,127]{2,1,0:T(8,128)}, f32[32,64,127]{2,1,0:T(8,128)}) fusion(f32[32,64,128]{2,1,0:T(8,128)} %param.4), kind=kLoop, calls=%fused_computation.356 | loop fusion | bytes 4161536 | tf_op jit(solution)/shard_map/slice | solution.py:55
  18.6 3.3 %collective-permute-start.3 = (f32[34,1,128]{2,1,0:T(1,128)S(1)}, f32[34,1,128]{2,1,0:T(1,128)S(1)}, u32[]{:S(2)}, u32[]{:S(2)}) collective-permute-start(f32[34,1,128]{2,1,0:T(1,128)S(1)} %get-tuple-element.103), channel_id=1, source_target_pairs={{0,1},{1,2},{2,3},{3,4},{4,5},{5,6},{6,7},{7,8},{8,9},{9,10},{10,1... | collective-permute-start | bytes 52232 | tf_op jit(solution)/shard_map/ppermute | solution.py:15
  21.9 2.4 %collective-permute-start.5 = (f32[34,1,128]{2,1,0:T(1,128)S(1)}, f32[34,1,128]{2,1,0:T(1,128)S(1)}, u32[]{:S(2)}, u32[]{:S(2)}) collective-permute-start(f32[34,1,128]{2,1,0:T(1,128)S(1)} %get-tuple-element.104), channel_id=1, source_target_pairs={{1,0},{2,1},{3,2},{4,3},{5,4},{6,5},{7,6},{8,7},{9,8},{10,9},{11,1... | collective-permute-start | bytes 52232 | tf_op jit(solution)/shard_map/ppermute | solution.py:17
  24.6 2.4 %collective-permute-done.5 = f32[34,1,128]{2,1,0:T(1,128)S(1)} collective-permute-done((f32[34,1,128]{2,1,0:T(1,128)S(1)}, f32[34,1,128]{2,1,0:T(1,128)S(1)}, u32[]{:S(2)}, u32[]{:S(2)}) %collective-permute-start.5) | collective-permute-done | bytes 17440 | tf_op jit(solution)/shard_map/ppermute | solution.py:17
  29.6 2.7 %collective-permute-start.6 = (f32[3,64,128]{2,1,0:T(8,128)S(1)}, f32[3,64,128]{2,1,0:T(8,128)S(1)}, u32[]{:S(2)}, u32[]{:S(2)}) collective-permute-start(f32[3,64,128]{2,1,0:T(8,128)S(1)} %get-tuple-element.6), channel_id=1, source_target_pairs={{16,0},{32,16},{48,32},{64,48},{80,64},{96,80},{112,96},{128,112},... | collective-permute-start | bytes 294920 | tf_op jit(solution)/shard_map/ppermute | solution.py:27
  32.9 3.2 %collective-permute-done.6 = f32[3,64,128]{2,1,0:T(8,128)S(1)} collective-permute-done((f32[3,64,128]{2,1,0:T(8,128)S(1)}, f32[3,64,128]{2,1,0:T(8,128)S(1)}, u32[]{:S(2)}, u32[]{:S(2)}) %collective-permute-start.6) | collective-permute-done | bytes 98336 | tf_op jit(solution)/shard_map/ppermute | solution.py:27
  36.1 3.4 %collective-permute-start.7 = (f32[4,64,128]{2,1,0:T(8,128)S(1)}, f32[4,64,128]{2,1,0:T(8,128)S(1)}, u32[]{:S(2)}, u32[]{:S(2)}) collective-permute-start(f32[4,64,128]{2,1,0:T(8,128)S(1)} %pad_maximum_fusion.6), channel_id=1, source_target_pairs={{0,16},{16,32},{32,48},{48,64},{64,80},{80,96},{96,112},{112,128},... | collective-permute-start | bytes 393224 | tf_op jit(solution)/shard_map/ppermute | solution.py:27
  39.6 4.6 %collective-permute-start.8 = (f32[4,64,128]{2,1,0:T(8,128)S(1)}, f32[4,64,128]{2,1,0:T(8,128)S(1)}, u32[]{:S(2)}, u32[]{:S(2)}) collective-permute-start(f32[4,64,128]{2,1,0:T(8,128)S(1)} %pad_maximum_fusion.6), channel_id=1, source_target_pairs={{16,0},{32,16},{48,32},{64,48},{80,64},{96,80},{112,96},{128,112},... | collective-permute-start | bytes 393224 | tf_op jit(solution)/shard_map/ppermute | solution.py:27
  45.1 1.5 %collective-permute-done.8 = f32[4,64,128]{2,1,0:T(8,128)S(1)} collective-permute-done((f32[4,64,128]{2,1,0:T(8,128)S(1)}, f32[4,64,128]{2,1,0:T(8,128)S(1)}, u32[]{:S(2)}, u32[]{:S(2)}) %collective-permute-start.8) | collective-permute-done | bytes 131104 | tf_op jit(solution)/shard_map/ppermute | solution.py:27
  46.7 4.8 %collective-permute-start.9 = (f32[4,64,128]{2,1,0:T(8,128)S(1)}, f32[4,64,128]{2,1,0:T(8,128)S(1)}, u32[]{:S(2)}, u32[]{:S(2)}) collective-permute-start(f32[4,64,128]{2,1,0:T(8,128)S(1)} %pad_maximum_fusion.7), channel_id=1, source_target_pairs={{0,32},{16,48},{32,64},{48,80},{64,96},{80,112},{96,128},{112,144}... | collective-permute-start | bytes 393224 | tf_op jit(solution)/shard_map/ppermute | solution.py:27
  51.5 3.4 %collective-permute-start.10 = (f32[4,64,128]{2,1,0:T(8,128)S(1)}, f32[4,64,128]{2,1,0:T(8,128)S(1)}, u32[]{:S(2)}, u32[]{:S(2)}) collective-permute-start(f32[4,64,128]{2,1,0:T(8,128)S(1)} %pad_maximum_fusion.7), channel_id=1, source_target_pairs={{32,0},{48,16},{64,32},{80,48},{96,64},{112,80},{128,96},{144,112}... | collective-permute-start | bytes 393224 | tf_op jit(solution)/shard_map/ppermute | solution.py:27
  55.0 1.9 %collective-permute-done.9 = f32[4,64,128]{2,1,0:T(8,128)S(1)} collective-permute-done((f32[4,64,128]{2,1,0:T(8,128)S(1)}, f32[4,64,128]{2,1,0:T(8,128)S(1)}, u32[]{:S(2)}, u32[]{:S(2)}) %collective-permute-start.9) | collective-permute-done | bytes 131104 | tf_op jit(solution)/shard_map/ppermute | solution.py:27
  56.9 4.3 %collective-permute-done.10 = f32[4,64,128]{2,1,0:T(8,128)S(1)} collective-permute-done((f32[4,64,128]{2,1,0:T(8,128)S(1)}, f32[4,64,128]{2,1,0:T(8,128)S(1)}, u32[]{:S(2)}, u32[]{:S(2)}) %collective-permute-start.10) | collective-permute-done | bytes 131104 | tf_op jit(solution)/shard_map/ppermute | solution.py:27
  61.3 3.5 %collective-permute-start.11 = (f32[4,64,128]{2,1,0:T(8,128)S(1)}, f32[4,64,128]{2,1,0:T(8,128)S(1)}, u32[]{:S(2)}, u32[]{:S(2)}) collective-permute-start(f32[4,64,128]{2,1,0:T(8,128)S(1)} %pad_maximum_fusion.8), channel_id=1, source_target_pairs={{0,64},{16,80},{32,96},{48,112},{64,128},{80,144},{96,160},{112,17... | collective-permute-start | bytes 393224 | tf_op jit(solution)/shard_map/ppermute | solution.py:27
  64.8 2.4 %collective-permute-start.12 = (f32[4,64,128]{2,1,0:T(8,128)S(1)}, f32[4,64,128]{2,1,0:T(8,128)S(1)}, u32[]{:S(2)}, u32[]{:S(2)}) collective-permute-start(f32[4,64,128]{2,1,0:T(8,128)S(1)} %pad_maximum_fusion.8), channel_id=1, source_target_pairs={{64,0},{80,16},{96,32},{112,48},{128,64},{144,80},{160,96},{176,11... | collective-permute-start | bytes 393224 | tf_op jit(solution)/shard_map/ppermute | solution.py:27
  67.1 1.4 %collective-permute-done.11 = f32[4,64,128]{2,1,0:T(8,128)S(1)} collective-permute-done((f32[4,64,128]{2,1,0:T(8,128)S(1)}, f32[4,64,128]{2,1,0:T(8,128)S(1)}, u32[]{:S(2)}, u32[]{:S(2)}) %collective-permute-start.11) | collective-permute-done | bytes 131104 | tf_op jit(solution)/shard_map/ppermute | solution.py:27
  68.6 4.2 %collective-permute-done.12 = f32[4,64,128]{2,1,0:T(8,128)S(1)} collective-permute-done((f32[4,64,128]{2,1,0:T(8,128)S(1)}, f32[4,64,128]{2,1,0:T(8,128)S(1)}, u32[]{:S(2)}, u32[]{:S(2)}) %collective-permute-start.12) | collective-permute-done | bytes 131104 | tf_op jit(solution)/shard_map/ppermute | solution.py:27
  72.8 8.1 %collective-permute-start.13 = (f32[4,64,128]{2,1,0:T(8,128)S(1)}, f32[4,64,128]{2,1,0:T(8,128)S(1)}, u32[]{:S(2)}, u32[]{:S(2)}) collective-permute-start(f32[4,64,128]{2,1,0:T(8,128)S(1)} %pad_maximum_fusion.9), channel_id=1, source_target_pairs={{0,128},{16,144},{32,160},{48,176},{64,192},{80,208},{96,224},{112... | collective-permute-start | bytes 393224 | tf_op jit(solution)/shard_map/ppermute | solution.py:27
  81.0 1.3 %collective-permute-start.14 = (f32[4,64,128]{2,1,0:T(8,128)S(1)}, f32[4,64,128]{2,1,0:T(8,128)S(1)}, u32[]{:S(2)}, u32[]{:S(2)}) collective-permute-start(f32[4,64,128]{2,1,0:T(8,128)S(1)} %pad_maximum_fusion.9), channel_id=1, source_target_pairs={{128,0},{144,16},{160,32},{176,48},{192,64},{208,80},{224,96},{240... | collective-permute-start | bytes 393224 | tf_op jit(solution)/shard_map/ppermute | solution.py:27
  82.3 2.2 %collective-permute-done.13 = f32[4,64,128]{2,1,0:T(8,128)S(1)} collective-permute-done((f32[4,64,128]{2,1,0:T(8,128)S(1)}, f32[4,64,128]{2,1,0:T(8,128)S(1)}, u32[]{:S(2)}, u32[]{:S(2)}) %collective-permute-start.13) | collective-permute-done | bytes 131104 | tf_op jit(solution)/shard_map/ppermute | solution.py:27
  84.5 5.7 %collective-permute-done.14 = f32[4,64,128]{2,1,0:T(8,128)S(1)} collective-permute-done((f32[4,64,128]{2,1,0:T(8,128)S(1)}, f32[4,64,128]{2,1,0:T(8,128)S(1)}, u32[]{:S(2)}, u32[]{:S(2)}) %collective-permute-start.14) | collective-permute-done | bytes 131104 | tf_op jit(solution)/shard_map/ppermute | solution.py:27
  90.2 2.4 %collective-permute-start.15 = (f32[4,64,128]{2,1,0:T(8,128)S(1)}, f32[4,64,128]{2,1,0:T(8,128)S(1)}, u32[]{:S(2)}, u32[]{:S(2)}) collective-permute-start(f32[4,64,128]{2,1,0:T(8,128)S(1)} %pad_maximum_fusion.10), channel_id=1, source_target_pairs={{0,256},{16,272},{32,288},{48,304},{64,320},{80,336},{96,352},{112... | collective-permute-start | bytes 393224 | tf_op jit(solution)/shard_map/ppermute | solution.py:27
  92.6 1.3 %collective-permute-start.16 = (f32[4,64,128]{2,1,0:T(8,128)S(1)}, f32[4,64,128]{2,1,0:T(8,128)S(1)}, u32[]{:S(2)}, u32[]{:S(2)}) collective-permute-start(f32[4,64,128]{2,1,0:T(8,128)S(1)} %pad_maximum_fusion.10), channel_id=1, source_target_pairs={{256,0},{272,16},{288,32},{304,48},{320,64},{336,80},{352,96},{368... | collective-permute-start | bytes 393224 | tf_op jit(solution)/shard_map/ppermute | solution.py:27
  93.9 4.4 %collective-permute-done.15 = f32[4,64,128]{2,1,0:T(8,128)S(1)} collective-permute-done((f32[4,64,128]{2,1,0:T(8,128)S(1)}, f32[4,64,128]{2,1,0:T(8,128)S(1)}, u32[]{:S(2)}, u32[]{:S(2)}) %collective-permute-start.15) | collective-permute-done | bytes 131104 | tf_op jit(solution)/shard_map/ppermute | solution.py:27
  98.3 6.0 %collective-permute-done.16 = f32[4,64,128]{2,1,0:T(8,128)S(1)} collective-permute-done((f32[4,64,128]{2,1,0:T(8,128)S(1)}, f32[4,64,128]{2,1,0:T(8,128)S(1)}, u32[]{:S(2)}, u32[]{:S(2)}) %collective-permute-start.16) | collective-permute-done | bytes 131104 | tf_op jit(solution)/shard_map/ppermute | solution.py:27
  104.4 2.4 %collective-permute-start.17 = (f32[64,128]{1,0:T(8,128)S(1)}, f32[64,128]{1,0:T(8,128)S(1)}, u32[]{:S(2)}, u32[]{:S(2)}) collective-permute-start(f32[64,128]{1,0:T(8,128)S(1)} %fusion.55), channel_id=1, source_target_pairs={{0,16},{16,32},{32,48},{48,64},{64,80},{80,96},{96,112},{112,128},... | collective-permute-start | bytes 98312 | tf_op jit(solution)/shard_map/ppermute | solution.py:27
  106.9 5.5 %collective-permute-done.17 = f32[64,128]{1,0:T(8,128)S(1)} collective-permute-done((f32[64,128]{1,0:T(8,128)S(1)}, f32[64,128]{1,0:T(8,128)S(1)}, u32[]{:S(2)}, u32[]{:S(2)}) %collective-permute-start.17) | collective-permute-done | bytes 32800 | tf_op jit(solution)/shard_map/ppermute | solution.py:27
  112.7 1.0 pad_maximum_fusion.5
  (102 shorter events, 7.5 us)
Async XLA Ops:
  0.0 18.1 %copy-start.1 = (f32[32,64,128]{2,1,0:T(8,128)S(1)}, f32[32,64,128]{2,1,0:T(8,128)}, u32[]{:S(2)}) copy-start(f32[32,64,128]{2,1,0:T(8,128)} %param.5) | copy-start | bytes 3145732
  0.9 17.5 %collective-permute-start = (f32[1,64,128]{2,1,0:T(8,128)S(1)}, f32[1,64,128]{2,1,0:T(8,128)S(1)}, u32[]{:S(2)}, u32[]{:S(2)}) collective-permute-start(f32[1,64,128]{2,1,0:T(8,128)S(1)} %get-tuple-element.188), channel_id=1, source_target_pairs={{0,16},{16,32},{32,48},{48,64},{64,80},{80,96},{96,112},{112,128},... | collective-permute-start | bytes 98312 | tf_op jit(solution)/shard_map/ppermute | solution.py:15
  4.3 14.3 %collective-permute-start.2 = (f32[1,64,128]{2,1,0:T(8,128)S(1)}, f32[1,64,128]{2,1,0:T(8,128)S(1)}, u32[]{:S(2)}, u32[]{:S(2)}) collective-permute-start(f32[1,64,128]{2,1,0:T(8,128)S(1)} %get-tuple-element.187), channel_id=1, source_target_pairs={{16,0},{32,16},{48,32},{64,48},{80,64},{96,80},{112,96},{128,112},... | collective-permute-start | bytes 98312 | tf_op jit(solution)/shard_map/ppermute | solution.py:17
  9.6 14.7 %collective-permute-start.1 = (f32[1,64,128]{2,1,0:T(8,128)S(1)}, f32[1,64,128]{2,1,0:T(8,128)S(1)}, u32[]{:S(2)}, u32[]{:S(2)}) collective-permute-start(f32[1,64,128]{2,1,0:T(8,128)S(1)} %slice.495), channel_id=1, source_target_pairs={{16,0},{32,16},{48,32},{64,48},{80,64},{96,80},{112,96},{128,112},... | collective-permute-start | bytes 98312 | tf_op jit(solution)/shard_map/ppermute | solution.py:27
  12.7 5.5 %copy-start.5 = (f32[64,128]{1,0:T(8,128)S(1)}, f32[64,128]{1,0:T(8,128)}, u32[]{:S(2)}) copy-start(f32[64,128]{1,0:T(8,128)} %param.6) | copy-start | bytes 98308
  12.7 5.6 %copy-start.4 = (f32[64,128]{1,0:T(8,128)S(1)}, f32[64,128]{1,0:T(8,128)}, u32[]{:S(2)}) copy-start(f32[64,128]{1,0:T(8,128)} %param.7) | copy-start | bytes 98308
  12.7 5.7 %copy-start = (f32[32,64,128]{2,1,0:T(8,128)S(1)}, f32[32,64,128]{2,1,0:T(8,128)}, u32[]{:S(2)}) copy-start(f32[32,64,128]{2,1,0:T(8,128)} %param.4) | copy-start | bytes 3145732
  12.7 5.7 %collective-permute-start.4 = (f32[1,128]{1,0:T(1,128)S(1)}, f32[1,128]{1,0:T(1,128)S(1)}, u32[]{:S(2)}, u32[]{:S(2)}) collective-permute-start(f32[1,128]{1,0:T(1,128)S(1)} %slice.501), channel_id=1, source_target_pairs={{1,0},{2,1},{3,2},{4,3},{5,4},{6,5},{7,6},{8,7},{9,8},{10,9},{11,1... | collective-permute-start | bytes 1544 | tf_op jit(solution)/shard_map/ppermute | solution.py:27
  18.4 8.5 %copy-start.2 = (f32[32,64,127]{2,1,0:T(8,128)S(1)}, f32[32,64,127]{2,1,0:T(8,128)}, u32[]{:S(2)}) copy-start(f32[32,64,127]{2,1,0:T(8,128)} %get-tuple-element.185) | copy-start | bytes 3121156
  18.5 8.5 %copy-start.3 = (f32[32,64,127]{2,1,0:T(8,128)S(1)}, f32[32,64,127]{2,1,0:T(8,128)}, u32[]{:S(2)}) copy-start(f32[32,64,127]{2,1,0:T(8,128)} %get-tuple-element.186) | copy-start | bytes 3121156
  18.6 6.0 %collective-permute-start.3 = (f32[34,1,128]{2,1,0:T(1,128)S(1)}, f32[34,1,128]{2,1,0:T(1,128)S(1)}, u32[]{:S(2)}, u32[]{:S(2)}) collective-permute-start(f32[34,1,128]{2,1,0:T(1,128)S(1)} %get-tuple-element.103), channel_id=1, source_target_pairs={{0,1},{1,2},{2,3},{3,4},{4,5},{5,6},{6,7},{7,8},{8,9},{9,10},{10,1... | collective-permute-start | bytes 52232 | tf_op jit(solution)/shard_map/ppermute | solution.py:15
  21.9 5.0 %collective-permute-start.5 = (f32[34,1,128]{2,1,0:T(1,128)S(1)}, f32[34,1,128]{2,1,0:T(1,128)S(1)}, u32[]{:S(2)}, u32[]{:S(2)}) collective-permute-start(f32[34,1,128]{2,1,0:T(1,128)S(1)} %get-tuple-element.104), channel_id=1, source_target_pairs={{1,0},{2,1},{3,2},{4,3},{5,4},{6,5},{7,6},{8,7},{9,8},{10,9},{11,1... | collective-permute-start | bytes 52232 | tf_op jit(solution)/shard_map/ppermute | solution.py:17
  29.6 6.5 %collective-permute-start.6 = (f32[3,64,128]{2,1,0:T(8,128)S(1)}, f32[3,64,128]{2,1,0:T(8,128)S(1)}, u32[]{:S(2)}, u32[]{:S(2)}) collective-permute-start(f32[3,64,128]{2,1,0:T(8,128)S(1)} %get-tuple-element.6), channel_id=1, source_target_pairs={{16,0},{32,16},{48,32},{64,48},{80,64},{96,80},{112,96},{128,112},... | collective-permute-start | bytes 294920 | tf_op jit(solution)/shard_map/ppermute | solution.py:27
  36.1 9.0 %collective-permute-start.7 = (f32[4,64,128]{2,1,0:T(8,128)S(1)}, f32[4,64,128]{2,1,0:T(8,128)S(1)}, u32[]{:S(2)}, u32[]{:S(2)}) collective-permute-start(f32[4,64,128]{2,1,0:T(8,128)S(1)} %pad_maximum_fusion.6), channel_id=1, source_target_pairs={{0,16},{16,32},{32,48},{48,64},{64,80},{80,96},{96,112},{112,128},... | collective-permute-start | bytes 393224 | tf_op jit(solution)/shard_map/ppermute | solution.py:27
  39.6 7.1 %collective-permute-start.8 = (f32[4,64,128]{2,1,0:T(8,128)S(1)}, f32[4,64,128]{2,1,0:T(8,128)S(1)}, u32[]{:S(2)}, u32[]{:S(2)}) collective-permute-start(f32[4,64,128]{2,1,0:T(8,128)S(1)} %pad_maximum_fusion.6), channel_id=1, source_target_pairs={{16,0},{32,16},{48,32},{64,48},{80,64},{96,80},{112,96},{128,112},... | collective-permute-start | bytes 393224 | tf_op jit(solution)/shard_map/ppermute | solution.py:27
  46.7 10.2 %collective-permute-start.9 = (f32[4,64,128]{2,1,0:T(8,128)S(1)}, f32[4,64,128]{2,1,0:T(8,128)S(1)}, u32[]{:S(2)}, u32[]{:S(2)}) collective-permute-start(f32[4,64,128]{2,1,0:T(8,128)S(1)} %pad_maximum_fusion.7), channel_id=1, source_target_pairs={{0,32},{16,48},{32,64},{48,80},{64,96},{80,112},{96,128},{112,144}... | collective-permute-start | bytes 393224 | tf_op jit(solution)/shard_map/ppermute | solution.py:27
  51.5 9.7 %collective-permute-start.10 = (f32[4,64,128]{2,1,0:T(8,128)S(1)}, f32[4,64,128]{2,1,0:T(8,128)S(1)}, u32[]{:S(2)}, u32[]{:S(2)}) collective-permute-start(f32[4,64,128]{2,1,0:T(8,128)S(1)} %pad_maximum_fusion.7), channel_id=1, source_target_pairs={{32,0},{48,16},{64,32},{80,48},{96,64},{112,80},{128,96},{144,112}... | collective-permute-start | bytes 393224 | tf_op jit(solution)/shard_map/ppermute | solution.py:27
  61.3 7.3 %collective-permute-start.11 = (f32[4,64,128]{2,1,0:T(8,128)S(1)}, f32[4,64,128]{2,1,0:T(8,128)S(1)}, u32[]{:S(2)}, u32[]{:S(2)}) collective-permute-start(f32[4,64,128]{2,1,0:T(8,128)S(1)} %pad_maximum_fusion.8), channel_id=1, source_target_pairs={{0,64},{16,80},{32,96},{48,112},{64,128},{80,144},{96,160},{112,17... | collective-permute-start | bytes 393224 | tf_op jit(solution)/shard_map/ppermute | solution.py:27
  64.8 8.0 %collective-permute-start.12 = (f32[4,64,128]{2,1,0:T(8,128)S(1)}, f32[4,64,128]{2,1,0:T(8,128)S(1)}, u32[]{:S(2)}, u32[]{:S(2)}) collective-permute-start(f32[4,64,128]{2,1,0:T(8,128)S(1)} %pad_maximum_fusion.8), channel_id=1, source_target_pairs={{64,0},{80,16},{96,32},{112,48},{128,64},{144,80},{160,96},{176,11... | collective-permute-start | bytes 393224 | tf_op jit(solution)/shard_map/ppermute | solution.py:27
  72.8 11.6 %collective-permute-start.13 = (f32[4,64,128]{2,1,0:T(8,128)S(1)}, f32[4,64,128]{2,1,0:T(8,128)S(1)}, u32[]{:S(2)}, u32[]{:S(2)}) collective-permute-start(f32[4,64,128]{2,1,0:T(8,128)S(1)} %pad_maximum_fusion.9), channel_id=1, source_target_pairs={{0,128},{16,144},{32,160},{48,176},{64,192},{80,208},{96,224},{112... | collective-permute-start | bytes 393224 | tf_op jit(solution)/shard_map/ppermute | solution.py:27
  81.0 9.2 %collective-permute-start.14 = (f32[4,64,128]{2,1,0:T(8,128)S(1)}, f32[4,64,128]{2,1,0:T(8,128)S(1)}, u32[]{:S(2)}, u32[]{:S(2)}) collective-permute-start(f32[4,64,128]{2,1,0:T(8,128)S(1)} %pad_maximum_fusion.9), channel_id=1, source_target_pairs={{128,0},{144,16},{160,32},{176,48},{192,64},{208,80},{224,96},{240... | collective-permute-start | bytes 393224 | tf_op jit(solution)/shard_map/ppermute | solution.py:27
  90.2 8.1 %collective-permute-start.15 = (f32[4,64,128]{2,1,0:T(8,128)S(1)}, f32[4,64,128]{2,1,0:T(8,128)S(1)}, u32[]{:S(2)}, u32[]{:S(2)}) collective-permute-start(f32[4,64,128]{2,1,0:T(8,128)S(1)} %pad_maximum_fusion.10), channel_id=1, source_target_pairs={{0,256},{16,272},{32,288},{48,304},{64,320},{80,336},{96,352},{112... | collective-permute-start | bytes 393224 | tf_op jit(solution)/shard_map/ppermute | solution.py:27
  92.6 11.8 %collective-permute-start.16 = (f32[4,64,128]{2,1,0:T(8,128)S(1)}, f32[4,64,128]{2,1,0:T(8,128)S(1)}, u32[]{:S(2)}, u32[]{:S(2)}) collective-permute-start(f32[4,64,128]{2,1,0:T(8,128)S(1)} %pad_maximum_fusion.10), channel_id=1, source_target_pairs={{256,0},{272,16},{288,32},{304,48},{320,64},{336,80},{352,96},{368... | collective-permute-start | bytes 393224 | tf_op jit(solution)/shard_map/ppermute | solution.py:27
  104.4 7.9 %collective-permute-start.17 = (f32[64,128]{1,0:T(8,128)S(1)}, f32[64,128]{1,0:T(8,128)S(1)}, u32[]{:S(2)}, u32[]{:S(2)}) collective-permute-start(f32[64,128]{1,0:T(8,128)S(1)} %fusion.55), channel_id=1, source_target_pairs={{0,16},{16,32},{32,48},{48,64},{64,80},{80,96},{96,112},{112,128},... | collective-permute-start | bytes 98312 | tf_op jit(solution)/shard_map/ppermute | solution.py:27
where the time goes:
time: 114 us
  starting transfers between devices  58.3 us (51%)
  waiting for transfers between devices  43.7 us (38%)
  local copies, waits for them, and re-layouts  6.2 us (5%)
  other arithmetic  4.74 us (4%)
    ppermute x14, starting transfers between devices, shifted(): return lax.ppermute(block, axis, route)  44.7 us
    ppermute x14, waiting for transfers between devices, shifted(): return lax.ppermute(block, axis, route)  41.3 us
    ppermute x2, starting transfers between devices, with_halo(): lax.ppermute(head, axis, [((i + 1) % count, i) for i in range(ends)])  6.95 us
    ppermute x2, starting transfers between devices, with_halo(): lax.ppermute(tail, axis, [(i, (i + 1) % count) for i in range(ends)])  6.69 us
    slice x1, local copies, waits for them, and re-layouts, shards(): thermal_state_initial[:, :, :-1]  3.37 us
    ppermute x2, waiting for transfers between devices, with_halo(): lax.ppermute(head, axis, [((i + 1) % count, i) for i in range(ends)])  2.36 us
  transfers between devices with their start and end apart: 18, of which 13 were waited for; matrix products, arithmetic and copies ran while one was open for 5% of the time, Pallas kernels for 0%

commit v1 on v0

v1 whole, which is shorter than its diff:
```python
import functools

import jax
import jax.numpy as jnp
from jax import lax
from jax.experimental import pallas as pl
from jax.experimental.pallas import tpu as pltpu
from jax.sharding import PartitionSpec as P

MESH = pl.DeviceIdType.MESH
F32 = jnp.float32

NG = 32
NYZ = 16
GY, GX = 8, 4
L = 32
ROWS = 64
TILES = ROWS // 8
SOLVERS = (4, 1, 3, 5, 7, 29, 31, 28)


def ring_distance(a, n):
    return min(a, n - a)


OFFSETS = sorted(
    [(dy, dx) for dy in range(GY) for dx in range(GX) if (dy, dx) != (0, 0)],
    key=lambda o: -(ring_distance(o[0], GY) + ring_distance(o[1], GX)),
)


def reciprocal(x):
    g = pl.reciprocal(x, approx=True)
    return g * (2.0 - x * g)


def sweep_kernel(
    u_hbm, k_hbm, ky_hbm, kz_hbm, out_hbm,
    u, k, ky, kz, fl, fr, g, rg, edge, coef,
    send_up, send_down, from_below, from_above,
    a_send, a_recv, w_send, w_recv, out,
    load_sem, halo_send_sem, halo_recv_sem,
    a_send_sem, a_recv_sem, w_send_sem, w_recv_sem, store_sem,
):
    me = lax.axis_index("gx")
    z = lax.axis_index("yz")
    is_solver = functools.reduce(jnp.logical_or, [me == s for s in SOLVERS])
    tile = sum(jnp.where(me == s, t, 0) for t, s in enumerate(SOLVERS))
    row0 = pl.multiple_of(tile * 8, 8)
    barrier = pltpu.get_barrier_semaphore()

    pieces = [
        (u_hbm.at[:, pl.ds(0, 8)], u.at[:, pl.ds(0, 8)]),
        (u_hbm.at[:, pl.ds(56, 8)], u.at[:, pl.ds(56, 8)]),
        (ky_hbm, ky),
        (k_hbm, k),
        (u_hbm.at[:, pl.ds(8, 48)], u.at[:, pl.ds(8, 48)]),
        (kz_hbm, kz),
    ]
    loads = [pltpu.make_async_copy(s, d, load_sem.at[i]) for i, (s, d) in enumerate(pieces)]
    for c in loads:
        c.start()

    @pl.when(z > 0)
    def _():
        pl.semaphore_signal(barrier, inc=1, device_id=(me, z - 1), device_id_type=MESH)

    @pl.when(z < NYZ - 1)
    def _():
        pl.semaphore_signal(barrier, inc=1, device_id=(me, z + 1), device_id_type=MESH)

    my, mx = me // GX, me % GX

    def other(o):
        return lax.rem(my + o[0], GY) * GX + lax.rem(mx + o[1], GX)

    @pl.when(is_solver)
    def _():
        for o in OFFSETS:
            pl.semaphore_signal(barrier, inc=1, device_id=(other(o), z), device_id_type=MESH)

    loads[0].wait()
    loads[1].wait()
    loads[2].wait()
    for i in range(L):
        send_up[pl.ds(i, 1), :] = u[i, pl.ds(63, 1), :]
        send_down[pl.ds(i, 1), :] = u[i, pl.ds(0, 1), :]
    send_down[pl.ds(32, 8), :] = jnp.broadcast_to(ky[pl.ds(0, 1), :], (8, 128))
    greeted = jnp.where(z > 0, 1, 0) + jnp.where(z < NYZ - 1, 1, 0)
    greeted = greeted + jnp.where(is_solver, len(SOLVERS) - 1, len(SOLVERS))
    pl.semaphore_wait(barrier, greeted)

    up = pltpu.make_async_remote_copy(
        src_ref=send_up, dst_ref=from_below, send_sem=halo_send_sem.at[0],
        recv_sem=halo_recv_sem.at[0], device_id=(me, z + 1), device_id_type=MESH,
    )
    down = pltpu.make_async_remote_copy(
        src_ref=send_down, dst_ref=from_above, send_sem=halo_send_sem.at[1],
        recv_sem=halo_recv_sem.at[1], device_id=(me, z - 1), device_id_type=MESH,
    )

    @pl.when(z < NYZ - 1)
    def _():
        up.start()

    @pl.when(z > 0)
    def _():
        down.start()

    @pl.when(z == 0)
    def _():
        from_below[...] = jnp.zeros((L, 128), F32)

    @pl.when(z == NYZ - 1)
    def _():
        from_above[...] = jnp.zeros((L + 8, 128), F32)

    loads[3].wait()
    zero = jnp.zeros((ROWS, 128), F32)

    def eliminate(i, state):
        link, mass, mass_p = state
        k_next = 0.5 * k[i]
        gi = reciprocal((k_next + mass) + link)
        left = link * gi
        right = k_next * gi
        fl[i - 1] = left
        fr[i - 1] = right
        g[i - 1] = gi
        return link * right, 1.0 + right * mass, mass_p + left * mass

    link, mass, mass_p = lax.fori_loop(1, L, eliminate, (0.5 * k[0], zero + 1.0, zero))
    for t in range(TILES):
        rows = slice(8 * t, 8 * t + 8)
        a_send[t, 0] = mass_p[rows]
        a_send[t, 1] = mass[rows]
        a_send[t, 2] = link[rows]

    loads[4].wait()
    loads[5].wait()
    row = lax.broadcasted_iota(jnp.int32, (ROWS, 128), 0)
    lane = lax.broadcasted_iota(jnp.int32, (ROWS, 128), 1)
    kya = jnp.where(row == ROWS - 1, 0.0, pltpu.roll(ky[...], ROWS - 1, 0))
    kza = jnp.where(lane == 127, 0.0, pltpu.roll(kz[...], 127, 1))
    coef[0] = 2.0 - ky[...] - kya - kz[...] - kza
    coef[1] = jnp.where(row == 0, 0.0, ky[...])
    coef[2] = kya
    coef[3] = jnp.where(lane == 0, 0.0, kz[...])
    coef[4] = kza

    def rhs(i):
        v = u[i]
        b = coef[0] * v
        b = b + coef[1] * pltpu.roll(v, 1, 0) + coef[2] * pltpu.roll(v, ROWS - 1, 0)
        b = b + coef[3] * pltpu.roll(v, 1, 1) + coef[4] * pltpu.roll(v, 127, 1)
        edge[i, pl.ds(0, 8)] = b[0:8]
        edge[i, pl.ds(8, 8)] = b[56:64]
        return b

    mid = pl.ds(8, 48)

    def source(i, state):
        r, r_p = state
        r = rhs(i)[8:56] + fr[i - 1, mid] * r
        rg[i, mid] = r * g[i, mid]
        return r, r_p + fl[i, mid] * r

    r = rhs(0)[8:56]
    rg[0, mid] = r * g[0, mid]
    r, r_p = lax.fori_loop(1, L - 1, source, (r, fl[0, mid] * r))
    r = rhs(L - 1)[8:56] + fr[L - 2, mid] * r
    for t in range(1, TILES - 1):
        rows = slice(8 * t - 8, 8 * t)
        a_send[t, 3] = r_p[rows]
        a_send[t, 4] = r[rows]

    def send_tile(t):
        @pl.when(me != SOLVERS[t])
        def _():
            pltpu.make_async_remote_copy(
                src_ref=a_send.at[t], dst_ref=a_recv.at[me], send_sem=a_send_sem,
                recv_sem=a_recv_sem, device_id=(SOLVERS[t], z), device_id_type=MESH,
            ).start()

        @pl.when(me == SOLVERS[t])
        def _():
            a_recv[me] = a_send[t]

    for t in range(TILES - 2, 0, -1):
        send_tile(t)

    @pl.when(z > 0)
    def _():
        up.wait_recv()

    @pl.when(z < NYZ - 1)
    def _():
        down.wait_recv()

    row8 = lax.broadcasted_iota(jnp.int32, (8, 128), 0)
    c_first = jnp.where(row8 == 0, jnp.broadcast_to(ky[pl.ds(0, 1), :], (8, 128)), 0.0)
    c_last = jnp.where(row8 == 7, from_above[pl.ds(32, 8), :], 0.0)
    first, last = pl.ds(0, 8), pl.ds(56, 8)

    def edge_rhs(i):
        b_first = edge[i, pl.ds(0, 8)] + c_first * from_below[pl.ds(i, 1), :]
        b_last = edge[i, pl.ds(8, 8)] + c_last * (from_above[pl.ds(i, 1), :] - u[i, last])
        return b_first, b_last

    def edge_source(i, state):
        r0, r7, p0, p7 = state
        b0, b7 = edge_rhs(i)
        r0 = b0 + fr[i - 1, first] * r0
        r7 = b7 + fr[i - 1, last] * r7
        rg[i, first] = r0 * g[i, first]
        rg[i, last] = r7 * g[i, last]
        return r0, r7, p0 + fl[i, first] * r0, p7 + fl[i, last] * r7

    r0, r7 = edge_rhs(0)
    rg[0, first] = r0 * g[0, first]
    rg[0, last] = r7 * g[0, last]
    r0, r7, p0, p7 = lax.fori_loop(
        1, L - 1, edge_source, (r0, r7, fl[0, first] * r0, fl[0, last] * r7)
    )
    b0, b7 = edge_rhs(L - 1)
    a_send[0, 3] = p0
    a_send[0, 4] = b0 + fr[L - 2, first] * r0
    a_send[TILES - 1, 3] = p7
    a_send[TILES - 1, 4] = b7 + fr[L - 2, last] * r7
    send_tile(0)
    send_tile(TILES - 1)

    @pl.when(is_solver)
    def _():
        landed = a_recv.at[pl.ds(0, NG - 1)]
        pltpu.make_async_copy(landed, landed, a_recv_sem).wait()
        masses = [a_recv[d, 1] + (a_recv[d + 1, 0] if d < NG - 1 else 0.0) for d in range(NG)]
        sources = [a_recv[d, 4] + (a_recv[d + 1, 3] if d < NG - 1 else 0.0) for d in range(NG)]
        links = [a_recv[d, 2] for d in range(NG)]
        ids = list(range(NG))
        levels = []
        while len(ids) > 1:
            gone = []
            new_links = []
            for j in range(0, len(ids), 2):
                gi = reciprocal((links[j] + links[j + 1]) + masses[j])
                left, right = links[j] * gi, links[j + 1] * gi
                gone.append((ids[j], left, right, sources[j] * gi))
                if j > 0:
                    masses[j - 1] = masses[j - 1] + left * masses[j]
                    sources[j - 1] = sources[j - 1] + left * sources[j]
                masses[j + 1] = masses[j + 1] + right * masses[j]
                sources[j + 1] = sources[j + 1] + right * sources[j]
                new_links.append(links[j] * right)
            levels.append((gone, ids[1::2]))
            ids, masses, sources, links = ids[1::2], masses[1::2], sources[1::2], new_links
        w = {-1: jnp.zeros((8, 128), F32), ids[0]: sources[0] * reciprocal(masses[0] + links[0])}
        for gone, kept in reversed(levels):
            for j, (d, left, right, part) in enumerate(gone):
                below = kept[j - 1] if j > 0 else -1
                w[d] = left * w[below] + right * w[kept[j]] + part
        for d in range(-1, NG):
            w_send[d + 1] = w[d]
        for o in OFFSETS:
            d = other(o)
            pltpu.make_async_remote_copy(
                src_ref=w_send.at[pl.ds(d, 2)], dst_ref=w_recv.at[:, pl.ds(row0, 8)],
                send_sem=w_send_sem, recv_sem=w_recv_sem, device_id=(d, z), device_id_type=MESH,
            ).start()
        w_recv[:, pl.ds(row0, 8), :] = w_send[pl.ds(me, 2)]
        landed = w_recv.at[:, pl.ds(0, ROWS - 8)]
        pltpu.make_async_copy(landed, landed, w_recv_sem).wait()

    @pl.when(jnp.logical_not(is_solver))
    def _():
        pltpu.make_async_copy(w_recv, w_recv, w_recv_sem).wait()

    w_p = w_recv[0]
    w_last = w_recv[1]
    out[L - 1] = w_last - u[L - 1]
    chunk = 8

    def back(j, w):
        i = L - 2 - j
        w = (fl[i] * w_p + rg[i]) + fr[i] * w
        out[i] = w - u[i]
        return w

    w = w_last
    stores = []
    for c in range(L // chunk):
        low = c * chunk - (1 if c > 0 else 0)
        w = lax.fori_loop(low, (c + 1) * chunk - 1, back, w)
        part = pl.ds(L - chunk * (c + 1), chunk)
        stores.append(pltpu.make_async_copy(out.at[part], out_hbm.at[part], store_sem.at[c]))
        stores[-1].start()

    @pl.when(z < NYZ - 1)
    def _():
        up.wait_send()

    @pl.when(z > 0)
    def _():
        down.wait_send()

    @pl.when(is_solver)
    def _():
        sent = a_send.at[pl.ds(0, TILES - 1)]
        pltpu.make_async_copy(sent, sent, a_send_sem).wait()
        sent = a_recv.at[pl.ds(0, NG - 1), pl.ds(0, 2)]
        pltpu.make_async_copy(sent, sent, w_send_sem).wait()

    @pl.when(jnp.logical_not(is_solver))
    def _():
        pltpu.make_async_copy(a_send, a_send, a_send_sem).wait()

    for c in stores:
        c.wait()


def shards(u, kx, ky, kz):
    field = pltpu.VMEM((L, ROWS, 128), F32)
    any_space = pl.BlockSpec(memory_space=pl.ANY)
    return pl.pallas_call(
        sweep_kernel,
        out_shape=jax.ShapeDtypeStruct((L, ROWS, 128), F32),
        in_specs=[any_space] * 4,
        out_specs=any_space,
        scratch_shapes=[
            field, field, pltpu.VMEM((ROWS, 128), F32), pltpu.VMEM((ROWS, 128), F32),
            field, field, field, field,
            pltpu.VMEM((L, 16, 128), F32), pltpu.VMEM((5, ROWS, 128), F32),
            pltpu.VMEM((L, 128), F32), pltpu.VMEM((L + 8, 128), F32),
            pltpu.VMEM((L, 128), F32), pltpu.VMEM((L + 8, 128), F32),
            pltpu.VMEM((TILES, 5, 8, 128), F32), pltpu.VMEM((NG, 5, 8, 128), F32),
            pltpu.VMEM((NG + 1, 8, 128), F32), pltpu.VMEM((2, ROWS, 128), F32),
            field,
            pltpu.SemaphoreType.DMA((6,)), pltpu.SemaphoreType.DMA((2,)),
            pltpu.SemaphoreType.DMA((2,)),
            pltpu.SemaphoreType.DMA, pltpu.SemaphoreType.DMA,
            pltpu.SemaphoreType.DMA, pltpu.SemaphoreType.DMA,
            pltpu.SemaphoreType.DMA((L // 8,)),
        ],
        compiler_params=pltpu.CompilerParams(
            collective_id=0, has_side_effects=True, vmem_limit_bytes=32 * 1024 * 1024
        ),
        name="implicit_sweep",
    )(u, kx, ky, kz)


def solution(mesh):
    return jax.shard_map(
        shards,
        mesh=mesh,
        in_specs=(P("gx", "yz", None), P("gx", "yz", None), P("yz", None), P("yz", None)),
        out_specs=P("gx", "yz", None),
        check_vma=False,
    )
```

time: 114 us -> 35.2 us (0.31)
  the two profiles are of different devices: /device:TPU:200 before, /device:TPU:384 now
where the time goes in v1:
time: 35.2 us; the launch traced here: 34.9 us
  Pallas kernels  29.9 us (85%)
  local copies, waits for them, and re-layouts  4.94 us (14%)
    pallas_call x1, Pallas kernels, shards(): pl.pallas_call(sweep_kernel, out_shape=jax.ShapeDtypeStruct((L, ROWS, 128...  29.9 us
    unnamed x9, local copies, waits for them, and re-layouts  4.94 us

profile of v1, /device:TPU:384, one launch (start us, length us, event | category | flops | bytes accessed | tf_op | source)
XLA Modules:
  0.0 34.9 jit_solution(8879808739767575164)
XLA Ops:
  0.0 0.0 copy-start
  0.0 1.2 %copy-done = f32[32,64,128]{2,1,0:T(8,128)S(1)} copy-done((f32[32,64,128]{2,1,0:T(8,128)S(1)}, f32[32,64,128]{2,1,0:T(8,128)}, u32[]{:S(2)}) %copy-start) | copy-done | bytes 1048600
  1.2 0.0 copy-start.1
  1.2 1.2 %copy-done.1 = f32[32,64,128]{2,1,0:T(8,128)S(1)} copy-done((f32[32,64,128]{2,1,0:T(8,128)S(1)}, f32[32,64,128]{2,1,0:T(8,128)}, u32[]{:S(2)}) %copy-start.1) | copy-done | bytes 1048600
  2.5 0.0 copy-start.2
  2.5 0.8 %copy-done.2 = f32[64,128]{1,0:T(8,128)S(1)} copy-done((f32[64,128]{1,0:T(8,128)S(1)}, f32[64,128]{1,0:T(8,128)}, u32[]{:S(2)}) %copy-start.2) | copy-done | bytes 32792
  3.2 0.0 copy-start.3
  3.2 0.8 %copy-done.3 = f32[64,128]{1,0:T(8,128)S(1)} copy-done((f32[64,128]{1,0:T(8,128)S(1)}, f32[64,128]{1,0:T(8,128)}, u32[]{:S(2)}) %copy-start.3) | copy-done | bytes 32792
  4.0 29.9 %implicit_sweep.1 = f32[32,64,128]{2,1,0:T(8,128)S(1)} custom-call(f32[32,64,128]{2,1,0:T(8,128)S(1)} %copy-done, f32[32,64,128]{2,1,0:T(8,128)S(1)} %copy-done.1, f32[64,128]{1,0:T(8,128)S(1)} %copy-done.2, f32[64,128]{1,0:T(8,128)S(1)} %copy-done.3), custom_call_target="tpu_custom_call" | custom-call | tf_op jit(solution)/shard_map/implicit_sweep/pallas_call | solution.py:324
  33.9 1.0 %copy.6 = f32[32,64,128]{2,1,0:T(8,128)} copy(f32[32,64,128]{2,1,0:T(8,128)S(1)} %implicit_sweep.1) | data formatting | bytes 2097152
Async XLA Ops:
  0.0 1.2 %copy-start = (f32[32,64,128]{2,1,0:T(8,128)S(1)}, f32[32,64,128]{2,1,0:T(8,128)}, u32[]{:S(2)}) copy-start(f32[32,64,128]{2,1,0:T(8,128)} %u_hbm.1) | copy-start | bytes 3145732
  1.2 1.2 %copy-start.1 = (f32[32,64,128]{2,1,0:T(8,128)S(1)}, f32[32,64,128]{2,1,0:T(8,128)}, u32[]{:S(2)}) copy-start(f32[32,64,128]{2,1,0:T(8,128)} %k_hbm.1) | copy-start | bytes 3145732
  2.5 0.8 %copy-start.2 = (f32[64,128]{1,0:T(8,128)S(1)}, f32[64,128]{1,0:T(8,128)}, u32[]{:S(2)}) copy-start(f32[64,128]{1,0:T(8,128)} %ky_hbm.1) | copy-start | bytes 98308
  3.2 0.8 %copy-start.3 = (f32[64,128]{1,0:T(8,128)S(1)}, f32[64,128]{1,0:T(8,128)}, u32[]{:S(2)}) copy-start(f32[64,128]{1,0:T(8,128)} %kz_hbm.1) | copy-start | bytes 98308

commit v2 on v1

--- a/solution.py
+++ b/solution.py
@@ -15,12 +15,19 @@
 GY, GX = 8, 4
 L = 32
 ROWS = 64
-TILES = ROWS // 8
-SOLVERS = (4, 1, 3, 5, 7, 29, 31, 28)
+SLOTS = 16
+WIDE = ROWS // SLOTS
 
 
 def ring_distance(a, n):
     return min(a, n - a)
+
+
+def distance_to_first(d):
+    return ring_distance(d // GX, GY) + ring_distance(d % GX, GX)
+
+
+SOLVERS = (4, 1, 3) + (2, 8, 24, 29) + tuple(d for d in range(NG) if distance_to_first(d) == 3) + (28,)
 
 
 OFFSETS = sorted(
@@ -35,18 +42,17 @@
 
 
 def sweep_kernel(
-    u_hbm, k_hbm, ky_hbm, kz_hbm, out_hbm,
-    u, k, ky, kz, fl, fr, g, rg, edge, coef,
+    u_hbm, k_hbm, ky_hbm, kz_hbm, out,
+    u, k, ky, kz, fl, fr, g, rg, planes,
     send_up, send_down, from_below, from_above,
-    a_send, a_recv, w_send, w_recv, out,
+    a_send, a_recv, w_send, w_recv,
     load_sem, halo_send_sem, halo_recv_sem,
-    a_send_sem, a_recv_sem, w_send_sem, w_recv_sem, store_sem,
+    a_send_sem, a_recv_sem, w_send_sem, w_recv_sem,
 ):
     me = lax.axis_index("gx")
     z = lax.axis_index("yz")
     is_solver = functools.reduce(jnp.logical_or, [me == s for s in SOLVERS])
-    tile = sum(jnp.where(me == s, t, 0) for t, s in enumerate(SOLVERS))
-    row0 = pl.multiple_of(tile * 8, 8)
+    slot = sum(jnp.where(me == d, s, 0) for s, d in enumerate(SOLVERS))
     barrier = pltpu.get_barrier_semaphore()
 
     pieces = [
@@ -115,6 +121,10 @@
     def _():
         from_above[...] = jnp.zeros((L + 8, 128), F32)
 
+    def put(part, plane):
+        for s in range(SLOTS):
+            a_send[s, part] = plane[WIDE * s : WIDE * (s + 1)]
+
     loads[3].wait()
     zero = jnp.zeros((ROWS, 128), F32)
 
@@ -130,11 +140,9 @@
         return link * right, 1.0 + right * mass, mass_p + left * mass
 
     link, mass, mass_p = lax.fori_loop(1, L, eliminate, (0.5 * k[0], zero + 1.0, zero))
-    for t in range(TILES):
-        rows = slice(8 * t, 8 * t + 8)
-        a_send[t, 0] = mass_p[rows]
-        a_send[t, 1] = mass[rows]
-        a_send[t, 2] = link[rows]
+    put(0, mass_p)
+    put(1, mass)
+    put(2, link)
 
     loads[4].wait()
     loads[5].wait()
@@ -142,52 +150,50 @@
     lane = lax.broadcasted_iota(jnp.int32, (ROWS, 128), 1)
     kya = jnp.where(row == ROWS - 1, 0.0, pltpu.roll(ky[...], ROWS - 1, 0))
     kza = jnp.where(lane == 127, 0.0, pltpu.roll(kz[...], 127, 1))
-    coef[0] = 2.0 - ky[...] - kya - kz[...] - kza
-    coef[1] = jnp.where(row == 0, 0.0, ky[...])
-    coef[2] = kya
-    coef[3] = jnp.where(lane == 0, 0.0, kz[...])
-    coef[4] = kza
-
-    def rhs(i):
-        v = u[i]
-        b = coef[0] * v
-        b = b + coef[1] * pltpu.roll(v, 1, 0) + coef[2] * pltpu.roll(v, ROWS - 1, 0)
-        b = b + coef[3] * pltpu.roll(v, 1, 1) + coef[4] * pltpu.roll(v, 127, 1)
-        edge[i, pl.ds(0, 8)] = b[0:8]
-        edge[i, pl.ds(8, 8)] = b[56:64]
-        return b
-
-    mid = pl.ds(8, 48)
+    planes[0] = 2.0 - ky[...] - kya - kz[...] - kza
+    planes[1] = jnp.where(row == 0, 0.0, ky[...])
+    planes[2] = kya
+    planes[3] = jnp.where(lane == 0, 0.0, kz[...])
+    planes[4] = kza
+
+    def rhs(j, _):
+        for i in range(4):
+            i = 4 * j + i
+            v = u[i]
+            b = planes[0] * v
+            b = b + planes[1] * pltpu.roll(v, 1, 0) + planes[2] * pltpu.roll(v, ROWS - 1, 0)
+            rg[i] = b + planes[3] * pltpu.roll(v, 1, 1) + planes[4] * pltpu.roll(v, 127, 1)
+        return 0
+
+    lax.fori_loop(0, L // 4, rhs, 0)
 
     def source(i, state):
         r, r_p = state
-        r = rhs(i)[8:56] + fr[i - 1, mid] * r
-        rg[i, mid] = r * g[i, mid]
-        return r, r_p + fl[i, mid] * r
-
-    r = rhs(0)[8:56]
-    rg[0, mid] = r * g[0, mid]
-    r, r_p = lax.fori_loop(1, L - 1, source, (r, fl[0, mid] * r))
-    r = rhs(L - 1)[8:56] + fr[L - 2, mid] * r
-    for t in range(1, TILES - 1):
-        rows = slice(8 * t - 8, 8 * t)
-        a_send[t, 3] = r_p[rows]
-        a_send[t, 4] = r[rows]
-
-    def send_tile(t):
-        @pl.when(me != SOLVERS[t])
+        r = rg[i] + fr[i - 1] * r
+        rg[i] = r * g[i]
+        return r, r_p + fl[i] * r
+
+    r = rg[0]
+    rg[0] = r * g[0]
+    r, r_p = lax.fori_loop(1, L - 1, source, (r, fl[0] * r))
+    r = rg[L - 1] + fr[L - 2] * r
+    put(3, r_p)
+    put(4, r)
+
+    def send_slot(s):
+        @pl.when(me != SOLVERS[s])
         def _():
             pltpu.make_async_remote_copy(
-                src_ref=a_send.at[t], dst_ref=a_recv.at[me], send_sem=a_send_sem,
-                recv_sem=a_recv_sem, device_id=(SOLVERS[t], z), device_id_type=MESH,
+                src_ref=a_send.at[s], dst_ref=a_recv.at[me], send_sem=a_send_sem,
+                recv_sem=a_recv_sem, device_id=(SOLVERS[s], z), device_id_type=MESH,
             ).start()
 
-        @pl.when(me == SOLVERS[t])
+        @pl.when(me == SOLVERS[s])
         def _():
-            a_recv[me] = a_send[t]
-
-    for t in range(TILES - 2, 0, -1):
-        send_tile(t)
+            a_recv[me] = a_send[s]
+
+    for s in range(SLOTS - 2, 0, -1):
+        send_slot(s)
 
     @pl.when(z > 0)
     def _():
@@ -200,35 +206,37 @@
     row8 = lax.broadcasted_iota(jnp.int32, (8, 128), 0)
     c_first = jnp.where(row8 == 0, jnp.broadcast_to(ky[pl.ds(0, 1), :], (8, 128)), 0.0)
     c_last = jnp.where(row8 == 7, from_above[pl.ds(32, 8), :], 0.0)
-    first, last = pl.ds(0, 8), pl.ds(56, 8)
+    first, last = pl.ds(0, 8), pl.ds(ROWS - 8, 8)
 
     def edge_rhs(i):
-        b_first = edge[i, pl.ds(0, 8)] + c_first * from_below[pl.ds(i, 1), :]
-        b_last = edge[i, pl.ds(8, 8)] + c_last * (from_above[pl.ds(i, 1), :] - u[i, last])
-        return b_first, b_last
+        b0 = c_first * from_below[pl.ds(i, 1), :]
+        b7 = c_last * (from_above[pl.ds(i, 1), :] - u[i, last])
+        return b0, b7
 
     def edge_source(i, state):
         r0, r7, p0, p7 = state
         b0, b7 = edge_rhs(i)
         r0 = b0 + fr[i - 1, first] * r0
         r7 = b7 + fr[i - 1, last] * r7
-        rg[i, first] = r0 * g[i, first]
-        rg[i, last] = r7 * g[i, last]
+        rg[i, first] += r0 * g[i, first]
+        rg[i, last] += r7 * g[i, last]
         return r0, r7, p0 + fl[i, first] * r0, p7 + fl[i, last] * r7
 
     r0, r7 = edge_rhs(0)
-    rg[0, first] = r0 * g[0, first]
-    rg[0, last] = r7 * g[0, last]
+    rg[0, first] += r0 * g[0, first]
+    rg[0, last] += r7 * g[0, last]
     r0, r7, p0, p7 = lax.fori_loop(
         1, L - 1, edge_source, (r0, r7, fl[0, first] * r0, fl[0, last] * r7)
     )
     b0, b7 = edge_rhs(L - 1)
-    a_send[0, 3] = p0
-    a_send[0, 4] = b0 + fr[L - 2, first] * r0
-    a_send[TILES - 1, 3] = p7
-    a_send[TILES - 1, 4] = b7 + fr[L - 2, last] * r7
-    send_tile(0)
-    send_tile(TILES - 1)
+    r0 = b0 + fr[L - 2, first] * r0
+    r7 = b7 + fr[L - 2, last] * r7
+    a_send[0, 3] += p0[:WIDE]
+    a_send[0, 4] += r0[:WIDE]
+    a_send[SLOTS - 1, 3] += p7[8 - WIDE :]
+    a_send[SLOTS - 1, 4] += r7[8 - WIDE :]
+    send_slot(0)
+    send_slot(SLOTS - 1)
 
     @pl.when(is_solver)
     def _():
@@ -254,7 +262,7 @@
                 new_links.append(links[j] * right)
             levels.append((gone, ids[1::2]))
             ids, masses, sources, links = ids[1::2], masses[1::2], sources[1::2], new_links
-        w = {-1: jnp.zeros((8, 128), F32), ids[0]: sources[0] * reciprocal(masses[0] + links[0])}
+        w = {-1: jnp.zeros((WIDE, 128), F32), ids[0]: sources[0] * reciprocal(masses[0] + links[0])}
         for gone, kept in reversed(levels):
             for j, (d, left, right, part) in enumerate(gone):
                 below = kept[j - 1] if j > 0 else -1
@@ -264,21 +272,23 @@
         for o in OFFSETS:
             d = other(o)
             pltpu.make_async_remote_copy(
-                src_ref=w_send.at[pl.ds(d, 2)], dst_ref=w_recv.at[:, pl.ds(row0, 8)],
+                src_ref=w_send.at[pl.ds(d, 2)], dst_ref=w_recv.at[slot],
                 send_sem=w_send_sem, recv_sem=w_recv_sem, device_id=(d, z), device_id_type=MESH,
             ).start()
-        w_recv[:, pl.ds(row0, 8), :] = w_send[pl.ds(me, 2)]
-        landed = w_recv.at[:, pl.ds(0, ROWS - 8)]
+        w_recv[slot] = w_send[pl.ds(me, 2)]
+        landed = w_recv.at[pl.ds(0, SLOTS - 1)]
         pltpu.make_async_copy(landed, landed, w_recv_sem).wait()
 
     @pl.when(jnp.logical_not(is_solver))
     def _():
         pltpu.make_async_copy(w_recv, w_recv, w_recv_sem).wait()
 
-    w_p = w_recv[0]
-    w_last = w_recv[1]
+    for s in range(SLOTS):
+        planes[0, pl.ds(WIDE * s, WIDE)] = w_recv[s, 0]
+        planes[1, pl.ds(WIDE * s, WIDE)] = w_recv[s, 1]
+    w_p = planes[0]
+    w_last = planes[1]
     out[L - 1] = w_last - u[L - 1]
-    chunk = 8
 
     def back(j, w):
         i = L - 2 - j
@@ -286,14 +296,7 @@
         out[i] = w - u[i]
         return w
 
-    w = w_last
-    stores = []
-    for c in range(L // chunk):
-        low = c * chunk - (1 if c > 0 else 0)
-        w = lax.fori_loop(low, (c + 1) * chunk - 1, back, w)
-        part = pl.ds(L - chunk * (c + 1), chunk)
-        stores.append(pltpu.make_async_copy(out.at[part], out_hbm.at[part], store_sem.at[c]))
-        stores[-1].start()
+    lax.fori_loop(0, L - 1, back, w_last)
 
     @pl.when(z < NYZ - 1)
     def _():
@@ -305,7 +308,7 @@
 
     @pl.when(is_solver)
     def _():
-        sent = a_send.at[pl.ds(0, TILES - 1)]
+        sent = a_send.at[pl.ds(0, SLOTS - 1)]
         pltpu.make_async_copy(sent, sent, a_send_sem).wait()
         sent = a_recv.at[pl.ds(0, NG - 1), pl.ds(0, 2)]
         pltpu.make_async_copy(sent, sent, w_send_sem).wait()
@@ -313,9 +316,6 @@
     @pl.when(jnp.logical_not(is_solver))
     def _():
         pltpu.make_async_copy(a_send, a_send, a_send_sem).wait()
-
-    for c in stores:
-        c.wait()
 
 
 def shards(u, kx, ky, kz):
@@ -323,29 +323,27 @@
     any_space = pl.BlockSpec(memory_space=pl.ANY)
     return pl.pallas_call(
         sweep_kernel,
-        out_shape=jax.ShapeDtypeStruct((L, ROWS, 128), F32),
+        out_shape=pltpu.VMEM((L, ROWS, 128), F32),
         in_specs=[any_space] * 4,
-        out_specs=any_space,
+        out_specs=pl.BlockSpec(memory_space=pltpu.VMEM),
         scratch_shapes=[
             field, field, pltpu.VMEM((ROWS, 128), F32), pltpu.VMEM((ROWS, 128), F32),
             field, field, field, field,
-            pltpu.VMEM((L, 16, 128), F32), pltpu.VMEM((5, ROWS, 128), F32),
+            pltpu.VMEM((5, ROWS, 128), F32),
             pltpu.VMEM((L, 128), F32), pltpu.VMEM((L + 8, 128), F32),
             pltpu.VMEM((L, 128), F32), pltpu.VMEM((L + 8, 128), F32),
-            pltpu.VMEM((TILES, 5, 8, 128), F32), pltpu.VMEM((NG, 5, 8, 128), F32),
-            pltpu.VMEM((NG + 1, 8, 128), F32), pltpu.VMEM((2, ROWS, 128), F32),
-            field,
+            pltpu.VMEM((SLOTS, 5, WIDE, 128), F32), pltpu.VMEM((NG, 5, WIDE, 128), F32),
+            pltpu.VMEM((NG + 1, WIDE, 128), F32), pltpu.VMEM((SLOTS, 2, WIDE, 128), F32),
             pltpu.SemaphoreType.DMA((6,)), pltpu.SemaphoreType.DMA((2,)),
             pltpu.SemaphoreType.DMA((2,)),
             pltpu.SemaphoreType.DMA, pltpu.SemaphoreType.DMA,
             pltpu.SemaphoreType.DMA, pltpu.SemaphoreType.DMA,
-            pltpu.SemaphoreType.DMA((L // 8,)),
         ],
         compiler_params=pltpu.CompilerParams(
             collective_id=0, has_side_effects=True, vmem_limit_bytes=32 * 1024 * 1024
         ),
         name="implicit_sweep",
-    )(u, kx, ky, kz)
+    )(*(pltpu.with_memory_space_constraint(a, pltpu.HBM) for a in (u, kx, ky, kz)))
 
 
 def solution(mesh):

time: 35.2 us -> 25.4 us (0.72)
  the two profiles are of different devices: /device:TPU:384 before, /device:TPU:1 now
where the time goes in v2:
time: 25.4 us; the launch traced here: 25.3 us
  Pallas kernels  24.3 us (96%)
  local copies, waits for them, and re-layouts  0.97 us (4%)
    pallas_call x1, Pallas kernels, shards(): pl.pallas_call(sweep_kernel, out_shape=pltpu.VMEM((L, ROWS, 128), F32), i...  24.3 us
    unnamed x1, local copies, waits for them, and re-layouts  0.97 us

profile of v2, /device:TPU:1, one launch (start us, length us, event | category | flops | bytes accessed | tf_op | source)
XLA Modules:
  0.0 25.3 jit_solution(3013195411480606966)
XLA Ops:
  0.0 24.3 %implicit_sweep.1 = f32[32,64,128]{2,1,0:T(8,128)S(1)} custom-call(f32[32,64,128]{2,1,0:T(8,128)} %u_hbm.1, f32[32,64,128]{2,1,0:T(8,128)} %k_hbm.1, f32[64,128]{1,0:T(8,128)} %ky_hbm.1, f32[64,128]{1,0:T(8,128)} %kz_hbm.1), custom_call_target="tpu_custom_call" | custom-call | tf_op jit(solution)/shard_map/implicit_sweep/pallas_call | solution.py:324
  24.3 1.0 %copy.6 = f32[32,64,128]{2,1,0:T(8,128)} copy(f32[32,64,128]{2,1,0:T(8,128)S(1)} %implicit_sweep.1) | data formatting | bytes 2097152

commit v3 on v2

v3 whole, which is shorter than its diff:
```python
import functools

import jax
import jax.numpy as jnp
from jax import lax
from jax.experimental import pallas as pl
from jax.experimental.pallas import tpu as pltpu
from jax.sharding import PartitionSpec as P

MESH = pl.DeviceIdType.MESH
F32 = jnp.float32

NG = 32
NYZ = 16
GY, GX = 8, 4
L = 32
ROWS = 64
SLOTS = 16
WIDE = ROWS // SLOTS
PART = 8
STEP = 4


def ring_distance(a, n):
    return min(a, n - a)


SOLVERS = (4, 1, 3, 8, 24, 29, 6, 9, 11, 12, 20, 25, 27, 30, 5, 28)


OFFSETS = sorted(
    [(dy, dx) for dy in range(GY) for dx in range(GX) if (dy, dx) != (0, 0)],
    key=lambda o: -(ring_distance(o[0], GY) + ring_distance(o[1], GX)),
)


def reciprocal(x):
    g = pl.reciprocal(x, approx=True)
    return g * (2.0 - x * g)


def planes_loop(low, high, body, state):
    def step(j, state):
        for i in range(STEP):
            state = body(low + STEP * j + i, state)
        return state

    return lax.fori_loop(0, (high - low) // STEP, step, state)


def sweep_kernel(
    u_hbm, k_hbm, ky_hbm, kz_hbm, out,
    u, k, ky, kz, fl, fr, g, rg, planes,
    send_up, send_down, from_below, from_above,
    a_send, a_recv, w_send, w_recv,
    load_sem, halo_send_sem, halo_recv_sem,
    a_send_sem, a_recv_sem, w_send_sem, w_recv_sem,
):
    me = lax.axis_index("gx")
    z = lax.axis_index("yz")
    my, mx = me // GX, me % GX
    is_solver = functools.reduce(jnp.logical_or, [me == s for s in SOLVERS])
    slot = sum(jnp.where(me == d, s, 0) for s, d in enumerate(SOLVERS))
    barrier = pltpu.get_barrier_semaphore()

    parts = [pl.ds(c, PART) for c in range(0, L, PART)]
    pieces = [(k_hbm.at[c], k.at[c]) for c in parts] + [(ky_hbm, ky), (kz_hbm, kz)]
    pieces += [(u_hbm.at[c], u.at[c]) for c in parts]
    loads = [pltpu.make_async_copy(s, d, load_sem.at[i]) for i, (s, d) in enumerate(pieces)]
    for c in loads:
        c.start()
    first_y, first_u = len(parts), len(parts) + 2

    @pl.when(z > 0)
    def _():
        pl.semaphore_signal(barrier, inc=1, device_id=(me, z - 1), device_id_type=MESH)

    @pl.when(z < NYZ - 1)
    def _():
        pl.semaphore_signal(barrier, inc=1, device_id=(me, z + 1), device_id_type=MESH)

    def other(o):
        return lax.rem(my + o[0], GY) * GX + lax.rem(mx + o[1], GX)

    @pl.when(is_solver)
    def _():
        for o in OFFSETS:
            pl.semaphore_signal(barrier, inc=1, device_id=(other(o), z), device_id_type=MESH)

    def put(part, plane):
        for s in range(SLOTS):
            a_send[s, part] = plane[WIDE * s : WIDE * (s + 1)]

    zero = jnp.zeros((ROWS, 128), F32)

    def eliminate(i, state):
        link, mass, mass_p = state
        k_next = 0.5 * k[i]
        gi = reciprocal((k_next + mass) + link)
        left = link * gi
        right = k_next * gi
        fl[i - 1] = left
        fr[i] = right
        g[i - 1] = gi
        return link * right, 1.0 + right * mass, mass_p + left * mass

    loads[0].wait()
    state = (0.5 * k[0], zero + 1.0, zero)
    for i in range(1, STEP):
        state = eliminate(i, state)
    state = planes_loop(STEP, PART, eliminate, state)
    for c in range(1, len(parts)):
        loads[c].wait()
        state = planes_loop(PART * c, PART * (c + 1), eliminate, state)
    link, mass, mass_p = state
    fr[0] = zero
    fl[L - 1] = zero
    g[L - 1] = zero
    put(0, mass_p)
    put(1, mass)
    put(2, link)

    loads[first_y].wait()
    loads[first_y + 1].wait()
    row = lax.broadcasted_iota(jnp.int32, (ROWS, 128), 0)
    lane = lax.broadcasted_iota(jnp.int32, (ROWS, 128), 1)
    kya = jnp.where(row == ROWS - 1, 0.0, pltpu.roll(ky[...], ROWS - 1, 0))
    kza = jnp.where(lane == 127, 0.0, pltpu.roll(kz[...], 127, 1))
    planes[0] = 2.0 - ky[...] - kya - kz[...] - kza
    planes[1] = jnp.where(row == 0, 0.0, ky[...])
    planes[2] = kya
    planes[3] = jnp.where(lane == 0, 0.0, kz[...])
    planes[4] = kza

    row8 = lax.broadcasted_iota(jnp.int32, (8, 128), 0)
    tiles = range(ROWS // 8)

    def source(j, state):
        r, r_p = list(state[: len(tiles)]), list(state[len(tiles) :])
        ids = [STEP * j + i for i in range(STEP)]
        v = [[u[i, pl.ds(8 * t, 8)] for t in tiles] for i in ids]
        from_above_row = [[pltpu.roll(v_t, 7, 0) for v_t in v_i] for v_i in v]
        from_below_row = [[pltpu.roll(v_t, 1, 0) for v_t in v_i] for v_i in v]
        for t in tiles:
            rows = pl.ds(8 * t, 8)
            c = [planes[n, rows] for n in range(5)]
            for n, i in enumerate(ids):
                x = v[n][t]
                below = from_below_row[n]
                above = from_above_row[n]
                below = below[t] if t == 0 else jnp.where(row8 == 0, below[t - 1], below[t])
                above = above[t] if t == tiles[-1] else jnp.where(row8 == 7, above[t + 1], above[t])
                b = c[0] * x + c[1] * below + c[2] * above
                b = b + c[3] * pltpu.roll(x, 1, 1) + c[4] * pltpu.roll(x, 127, 1)
                r[t] = b + fr[i, rows] * r[t]
                rg[i, rows] = r[t] * g[i, rows]
                r_p[t] = r_p[t] + fl[i, rows] * r[t]
        return (*r, *r_p)

    state = (jnp.zeros((8, 128), F32),) * (2 * len(tiles))
    for c in range(len(parts)):
        loads[first_u + c].wait()
        state = lax.fori_loop(c * PART // STEP, (c + 1) * PART // STEP, source, state)
    for t in tiles:
        for h in range(8 // WIDE):
            rows = slice(WIDE * h, WIDE * (h + 1))
            a_send[t * (8 // WIDE) + h, 3] = state[len(tiles) + t][rows]
            a_send[t * (8 // WIDE) + h, 4] = state[t][rows]

    for i in range(L):
        send_up[pl.ds(i, 1), :] = u[i, pl.ds(ROWS - 1, 1), :]
        send_down[pl.ds(i, 1), :] = u[i, pl.ds(0, 1), :]
    send_down[pl.ds(L, 8), :] = jnp.broadcast_to(ky[pl.ds(0, 1), :], (8, 128))
    up = pltpu.make_async_remote_copy(
        src_ref=send_up, dst_ref=from_below, send_sem=halo_send_sem.at[0],
        recv_sem=halo_recv_sem.at[0], device_id=(me, z + 1), device_id_type=MESH,
    )
    down = pltpu.make_async_remote_copy(
        src_ref=send_down, dst_ref=from_above, send_sem=halo_send_sem.at[1],
        recv_sem=halo_recv_sem.at[1], device_id=(me, z - 1), device_id_type=MESH,
    )

    @pl.when(z == 0)
    def _():
        from_below[...] = jnp.zeros((L, 128), F32)

    @pl.when(z == NYZ - 1)
    def _():
        from_above[...] = jnp.zeros((L + 8, 128), F32)

    greeted = jnp.where(z > 0, 1, 0) + jnp.where(z < NYZ - 1, 1, 0)
    greeted = greeted + jnp.where(is_solver, len(SOLVERS) - 1, len(SOLVERS))
    pl.semaphore_wait(barrier, greeted)
    pl.when(z < NYZ - 1)(up.start)
    pl.when(z > 0)(down.start)

    def send_slot(s, low, count):
        part = pl.ds(low, count)

        @pl.when(me != SOLVERS[s])
        def _():
            pltpu.make_async_remote_copy(
                src_ref=a_send.at[s, part], dst_ref=a_recv.at[me, part], send_sem=a_send_sem,
                recv_sem=a_recv_sem, device_id=(SOLVERS[s], z), device_id_type=MESH,
            ).start()

        @pl.when(me == SOLVERS[s])
        def _():
            a_recv[me, part] = a_send[s, part]

    for s in range(SLOTS - 2, 0, -1):
        send_slot(s, 0, 5)
    send_slot(0, 0, 3)
    send_slot(SLOTS - 1, 0, 3)

    @pl.when(z > 0)
    def _():
        up.wait_recv()

    @pl.when(z < NYZ - 1)
    def _():
        down.wait_recv()

    c_first = jnp.where(row8 == 0, jnp.broadcast_to(ky[pl.ds(0, 1), :], (8, 128)), 0.0)
    c_last = jnp.where(row8 == 7, from_above[pl.ds(32, 8), :], 0.0)
    first, last = pl.ds(0, 8), pl.ds(ROWS - 8, 8)

    def edge_source(i, state):
        r0, r7, p0, p7 = state
        b0 = c_first * from_below[pl.ds(i, 1), :]
        b7 = c_last * (from_above[pl.ds(i, 1), :] - u[i, last])
        r0 = b0 + fr[i, first] * r0
        r7 = b7 + fr[i, last] * r7
        rg[i, first] += r0 * g[i, first]
        rg[i, last] += r7 * g[i, last]
        return r0, r7, p0 + fl[i, first] * r0, p7 + fl[i, last] * r7

    zero8 = jnp.zeros((8, 128), F32)
    r0, r7, p0, p7 = planes_loop(0, L, edge_source, (zero8,) * 4)
    a_send[0, 3] += p0[:WIDE]
    a_send[0, 4] += r0[:WIDE]
    a_send[SLOTS - 1, 3] += p7[8 - WIDE :]
    a_send[SLOTS - 1, 4] += r7[8 - WIDE :]
    send_slot(0, 3, 2)
    send_slot(SLOTS - 1, 3, 2)

    @pl.when(is_solver)
    def _():
        landed = a_recv.at[pl.ds(0, NG - 1)]
        pltpu.make_async_copy(landed, landed, a_recv_sem).wait()
        masses = [a_recv[d, 1] + (a_recv[d + 1, 0] if d < NG - 1 else 0.0) for d in range(NG)]
        sources = [a_recv[d, 4] + (a_recv[d + 1, 3] if d < NG - 1 else 0.0) for d in range(NG)]
        links = [a_recv[d, 2] for d in range(NG)]
        ids = list(range(NG))
        levels = []
        while len(ids) > 1:
            gone = []
            new_links = []
            for j in range(0, len(ids), 2):
                gi = reciprocal((links[j] + links[j + 1]) + masses[j])
                left, right = links[j] * gi, links[j + 1] * gi
                gone.append((ids[j], left, right, sources[j] * gi))
                if j > 0:
                    masses[j - 1] = masses[j - 1] + left * masses[j]
                    sources[j - 1] = sources[j - 1] + left * sources[j]
                masses[j + 1] = masses[j + 1] + right * masses[j]
                sources[j + 1] = sources[j + 1] + right * sources[j]
                new_links.append(links[j] * right)
            levels.append((gone, ids[1::2]))
            ids, masses, sources, links = ids[1::2], masses[1::2], sources[1::2], new_links
        w = {-1: jnp.zeros((WIDE, 128), F32), ids[0]: sources[0] * reciprocal(masses[0] + links[0])}
        for gone, kept in reversed(levels):
            for j, (d, left, right, part) in enumerate(gone):
                below = kept[j - 1] if j > 0 else -1
                w[d] = left * w[below] + right * w[kept[j]] + part
        for d in range(-1, NG):
            w_send[d + 1] = w[d]
        for i in range(NG):
            d = NG // 2 * (i // (NG // 2)) + lax.rem(i + slot, NG // 2)

            @pl.when(d != me)
            def _():
                pltpu.make_async_remote_copy(
                    src_ref=w_send.at[pl.ds(d, 2)], dst_ref=w_recv.at[slot],
                    send_sem=w_send_sem, recv_sem=w_recv_sem, device_id=(d, z), device_id_type=MESH,
                ).start()

        w_recv[slot] = w_send[pl.ds(me, 2)]
        landed = w_recv.at[pl.ds(0, SLOTS - 1)]
        pltpu.make_async_copy(landed, landed, w_recv_sem).wait()

    @pl.when(jnp.logical_not(is_solver))
    def _():
        pltpu.make_async_copy(w_recv, w_recv, w_recv_sem).wait()

    for s in range(SLOTS):
        planes[0, pl.ds(WIDE * s, WIDE)] = w_recv[s, 0]
        planes[1, pl.ds(WIDE * s, WIDE)] = w_recv[s, 1]
    w_p = planes[0]
    w_last = planes[1]
    def back(j, w):
        i = L - 1 - j
        w = (fl[i] * w_p + rg[i]) + fr[i + 1] * w
        out[i] = w - u[i]
        return w

    out[L - 1] = w_last - u[L - 1]
    w = w_last
    for j in range(1, STEP):
        w = back(j, w)
    planes_loop(STEP, L, back, w)

    @pl.when(z < NYZ - 1)
    def _():
        up.wait_send()

    @pl.when(z > 0)
    def _():
        down.wait_send()

    @pl.when(is_solver)
    def _():
        sent = a_send.at[pl.ds(0, SLOTS - 1)]
        pltpu.make_async_copy(sent, sent, a_send_sem).wait()
        sent = a_recv.at[pl.ds(0, NG - 1), pl.ds(0, 2)]
        pltpu.make_async_copy(sent, sent, w_send_sem).wait()

    @pl.when(jnp.logical_not(is_solver))
    def _():
        pltpu.make_async_copy(a_send, a_send, a_send_sem).wait()


def shards(u, kx, ky, kz):
    field = pltpu.VMEM((L, ROWS, 128), F32)
    any_space = pl.BlockSpec(memory_space=pl.ANY)
    return pl.pallas_call(
        sweep_kernel,
        out_shape=pltpu.VMEM((L, ROWS, 128), F32),
        in_specs=[any_space] * 4,
        out_specs=pl.BlockSpec(memory_space=pltpu.VMEM),
        scratch_shapes=[
            field, field, pltpu.VMEM((ROWS, 128), F32), pltpu.VMEM((ROWS, 128), F32),
            field, field, field, field,
            pltpu.VMEM((5, ROWS, 128), F32),
            pltpu.VMEM((L, 128), F32), pltpu.VMEM((L + 8, 128), F32),
            pltpu.VMEM((L, 128), F32), pltpu.VMEM((L + 8, 128), F32),
            pltpu.VMEM((SLOTS, 5, WIDE, 128), F32), pltpu.VMEM((NG, 5, WIDE, 128), F32),
            pltpu.VMEM((NG + 1, WIDE, 128), F32), pltpu.VMEM((SLOTS, 2, WIDE, 128), F32),
            pltpu.SemaphoreType.DMA((2 + 2 * (L // PART),)), pltpu.SemaphoreType.DMA((2,)),
            pltpu.SemaphoreType.DMA((2,)),
            pltpu.SemaphoreType.DMA, pltpu.SemaphoreType.DMA,
            pltpu.SemaphoreType.DMA, pltpu.SemaphoreType.DMA,
        ],
        compiler_params=pltpu.CompilerParams(
            collective_id=0, has_side_effects=True, vmem_limit_bytes=32 * 1024 * 1024
        ),
        name="implicit_sweep",
    )(*(pltpu.with_memory_space_constraint(a, pltpu.HBM) for a in (u, kx, ky, kz)))


def solution(mesh):
    return jax.shard_map(
        shards,
        mesh=mesh,
        in_specs=(P("gx", "yz", None), P("gx", "yz", None), P("yz", None), P("yz", None)),
        out_specs=P("gx", "yz", None),
        check_vma=False,
    )
```

time: 25.4 us -> 22.3 us (0.88)
  Pallas kernels: 24.3 us -> 21.2 us
    pallas_call x1, Pallas kernels: 24.3 us -> 21.2 us  [shards(): pl.pallas_call(sweep_kernel, out_shape=pltpu.VMEM((L, ROWS, 128), F32), i...]
where the time goes in v3:
time: 22.3 us; the launch traced here: 22.2 us
  Pallas kernels  21.2 us (95%)
  local copies, waits for them, and re-layouts  0.97 us (4%)
    pallas_call x1, Pallas kernels, shards(): pl.pallas_call(sweep_kernel, out_shape=pltpu.VMEM((L, ROWS, 128), F32), i...  21.2 us
    unnamed x1, local copies, waits for them, and re-layouts  0.97 us

profile of v3, /device:TPU:1, one launch (start us, length us, event | category | flops | bytes accessed | tf_op | source)
XLA Modules:
  0.0 22.2 jit_solution(13881163563880294744)
XLA Ops:
  0.0 21.2 %implicit_sweep.1 = f32[32,64,128]{2,1,0:T(8,128)S(1)} custom-call(f32[32,64,128]{2,1,0:T(8,128)} %u_hbm.1, f32[32,64,128]{2,1,0:T(8,128)} %k_hbm.1, f32[64,128]{1,0:T(8,128)} %ky_hbm.1, f32[64,128]{1,0:T(8,128)} %kz_hbm.1), custom_call_target="tpu_custom_call" | custom-call | tf_op jit(solution)/shard_map/implicit_sweep/pallas_call | solution.py:336
  21.2 1.0 %copy.6 = f32[32,64,128]{2,1,0:T(8,128)} copy(f32[32,64,128]{2,1,0:T(8,128)S(1)} %implicit_sweep.1) | data formatting | bytes 2097152

commit v4 on v3

--- a/solution.py
+++ b/solution.py
@@ -49,8 +49,9 @@
 
 
 def sweep_kernel(
-    u_hbm, k_hbm, ky_hbm, kz_hbm, out,
-    u, k, ky, kz, fl, fr, g, rg, planes,
+    u_hbm, k_hbm, ky_hbm, kz_hbm,
+    u, fl, fr, rg, w,
+    k, ky, kz, g, planes,
     send_up, send_down, from_below, from_above,
     a_send, a_recv, w_send, w_recv,
     load_sem, halo_send_sem, halo_recv_sem,
@@ -268,13 +269,13 @@
                 new_links.append(links[j] * right)
             levels.append((gone, ids[1::2]))
             ids, masses, sources, links = ids[1::2], masses[1::2], sources[1::2], new_links
-        w = {-1: jnp.zeros((WIDE, 128), F32), ids[0]: sources[0] * reciprocal(masses[0] + links[0])}
+        value = {-1: jnp.zeros((WIDE, 128), F32), ids[0]: sources[0] * reciprocal(masses[0] + links[0])}
         for gone, kept in reversed(levels):
             for j, (d, left, right, part) in enumerate(gone):
                 below = kept[j - 1] if j > 0 else -1
-                w[d] = left * w[below] + right * w[kept[j]] + part
+                value[d] = left * value[below] + right * value[kept[j]] + part
         for d in range(-1, NG):
-            w_send[d + 1] = w[d]
+            w_send[d + 1] = value[d]
         for i in range(NG):
             d = NG // 2 * (i // (NG // 2)) + lax.rem(i + slot, NG // 2)
 
@@ -294,21 +295,8 @@
         pltpu.make_async_copy(w_recv, w_recv, w_recv_sem).wait()
 
     for s in range(SLOTS):
-        planes[0, pl.ds(WIDE * s, WIDE)] = w_recv[s, 0]
-        planes[1, pl.ds(WIDE * s, WIDE)] = w_recv[s, 1]
-    w_p = planes[0]
-    w_last = planes[1]
-    def back(j, w):
-        i = L - 1 - j
-        w = (fl[i] * w_p + rg[i]) + fr[i + 1] * w
-        out[i] = w - u[i]
-        return w
-
-    out[L - 1] = w_last - u[L - 1]
-    w = w_last
-    for j in range(1, STEP):
-        w = back(j, w)
-    planes_loop(STEP, L, back, w)
+        w[0, pl.ds(WIDE * s, WIDE)] = w_recv[s, 0]
+        w[1, pl.ds(WIDE * s, WIDE)] = w_recv[s, 1]
 
     @pl.when(z < NYZ - 1)
     def _():
@@ -330,18 +318,50 @@
         pltpu.make_async_copy(a_send, a_send, a_send_sem).wait()
 
 
+def back_kernel(u, fl, fr, rg, w, out_hbm, out, store_sem):
+    w_p = w[0]
+
+    def back(i, value):
+        value = (fl[i] * w_p + rg[i]) + fr[i + 1] * value
+        out[i] = value - u[i]
+        return value
+
+    value = w[1]
+    out[L - 1] = value - u[L - 1]
+    stores = []
+    for low in range(L - PART, -1, -PART):
+        top = low + PART - 1
+        if top == L - 1:
+            for i in range(top - 1, top - STEP, -1):
+                value = back(i, value)
+            top -= STEP
+
+        def step(j, value):
+            for i in range(STEP):
+                value = back(top - STEP * j - i, value)
+            return value
+
+        value = lax.fori_loop(0, (top + 1 - low) // STEP, step, value)
+        part = pl.ds(low, PART)
+        stores.append(pltpu.make_async_copy(out.at[part], out_hbm.at[part], store_sem.at[low // PART]))
+        stores[-1].start()
+    for c in stores:
+        c.wait()
+
+
 def shards(u, kx, ky, kz):
-    field = pltpu.VMEM((L, ROWS, 128), F32)
+    shape = (L, ROWS, 128)
+    field = pltpu.VMEM(shape, F32)
+    plane = pltpu.VMEM((ROWS, 128), F32)
     any_space = pl.BlockSpec(memory_space=pl.ANY)
-    return pl.pallas_call(
+    vmem = pl.BlockSpec(memory_space=pltpu.VMEM)
+    blocks = pl.pallas_call(
         sweep_kernel,
-        out_shape=pltpu.VMEM((L, ROWS, 128), F32),
+        out_shape=(field, field, field, field, pltpu.VMEM((2, ROWS, 128), F32)),
         in_specs=[any_space] * 4,
-        out_specs=pl.BlockSpec(memory_space=pltpu.VMEM),
+        out_specs=(vmem,) * 5,
         scratch_shapes=[
-            field, field, pltpu.VMEM((ROWS, 128), F32), pltpu.VMEM((ROWS, 128), F32),
-            field, field, field, field,
-            pltpu.VMEM((5, ROWS, 128), F32),
+            field, plane, plane, field, pltpu.VMEM((5, ROWS, 128), F32),
             pltpu.VMEM((L, 128), F32), pltpu.VMEM((L + 8, 128), F32),
             pltpu.VMEM((L, 128), F32), pltpu.VMEM((L + 8, 128), F32),
             pltpu.VMEM((SLOTS, 5, WIDE, 128), F32), pltpu.VMEM((NG, 5, WIDE, 128), F32),
@@ -352,10 +372,19 @@
             pltpu.SemaphoreType.DMA, pltpu.SemaphoreType.DMA,
         ],
         compiler_params=pltpu.CompilerParams(
-            collective_id=0, has_side_effects=True, vmem_limit_bytes=32 * 1024 * 1024
+            collective_id=0, has_side_effects=True, vmem_limit_bytes=24 * 1024 * 1024
         ),
         name="implicit_sweep",
     )(*(pltpu.with_memory_space_constraint(a, pltpu.HBM) for a in (u, kx, ky, kz)))
+    return pl.pallas_call(
+        back_kernel,
+        out_shape=pltpu.HBM(shape, F32),
+        in_specs=[vmem] * 5,
+        out_specs=any_space,
+        scratch_shapes=[field, pltpu.SemaphoreType.DMA((L // PART,))],
+        compiler_params=pltpu.CompilerParams(vmem_limit_bytes=16 * 1024 * 1024),
+        name="back_substitution",
+    )(*(pltpu.with_memory_space_constraint(a, pltpu.VMEM) for a in blocks))
 
 
 def solution(mesh):

time: 22.3 us -> 22.2 us (level)
  local copies, waits for them, and re-layouts: 0.97 us -> 0 us
  Pallas kernels: 21.2 us -> 22 us
    unnamed x1 -> x0, local copies, waits for them, and re-layouts: 0.97 us -> none
    pallas_call x1 -> x2, Pallas kernels: 21.2 us -> 22 us  [the longest x1 21 us: shards(): pl.pallas_call(sweep_kernel, out_shape=(field, field, field, field, pltpu...]
where the time goes in v4:
time: 22.2 us; the launch traced here: 22 us
  Pallas kernels  22 us (99%)
    pallas_call x1, Pallas kernels, shards(): pl.pallas_call(sweep_kernel, out_shape=(field, field, field, field, pltpu...  21 us
    pallas_call x1, Pallas kernels, shards(): pl.pallas_call(back_kernel, out_shape=pltpu.HBM(shape, F32), in_specs=[vm...  1.05 us

profile of v4, /device:TPU:1, one launch (start us, length us, event | category | flops | bytes accessed | tf_op | source)
XLA Modules:
  0.0 22.0 jit_solution(4532805258055526352)
XLA Ops:
  0.0 21.0 %implicit_sweep.1 = (f32[32,64,128]{2,1,0:T(8,128)S(1)}, f32[32,64,128]{2,1,0:T(8,128)S(1)}, f32[32,64,128]{2,1,0:T(8,128)S(1)}, f32[32,64,128]{2,1,0:T(8,128)S(1)}, f32[2,64,128]{2,1,0:T(8,128)S(1)}) custom-call(f32[32,64,128]{2,1,0:T(8,128)} %u_hbm.1, f32[32,64,128]{2,1,0:T(8,128)} %k_hbm.1, f32[64,128]{1,0:T(8,128)} %ky_hbm.1, f32[64,128]{1,0:T(8,128)} %kz_hbm.1), custom_call_target="tpu_custom_call" | custom-call | tf_op jit(solution)/shard_map/implicit_sweep/pallas_call | solution.py:358
  21.0 1.0 %back_substitution.1 = f32[32,64,128]{2,1,0:T(8,128)} custom-call(f32[32,64,128]{2,1,0:T(8,128)S(1)} %get-tuple-element.10.u, f32[32,64,128]{2,1,0:T(8,128)S(1)} %get-tuple-element.11.fl, f32[32,64,128]{2,1,0:T(8,128)S(1)} %get-tuple-element.12.fr, f32[32,64,128]{2,1,0:T(8,128)S(1)} %get-tuple-element.13.rg, f32[2,64,128]{2,1,0:T(8,128)S(1)} %get-tuple-element.14.w), custom_call_target="tpu_custom_call" | custom-call | tf_op jit(solution)/shard_map/back_substitution/pallas_call | solution.py:379

commit v5 on v4

--- a/solution.py
+++ b/solution.py
@@ -25,7 +25,7 @@
     return min(a, n - a)
 
 
-SOLVERS = (4, 1, 3, 8, 24, 29, 6, 9, 11, 12, 20, 25, 27, 30, 5, 28)
+SOLVERS = (1, 4, 28, 2, 24, 29, 6, 9, 11, 12, 20, 25, 16, 15, 13, 3)
 
 
 OFFSETS = sorted(

time: 22.2 us -> 21.9 us (0.986)
  the two profiles are of different devices: /device:TPU:1 before, /device:TPU:232 now
where the time goes in v5:
time: 21.9 us; the launch traced here: 21.8 us
  Pallas kernels  21.8 us (100%)
    pallas_call x1, Pallas kernels, shards(): pl.pallas_call(sweep_kernel, out_shape=(field, field, field, field, pltpu...  20.7 us
    pallas_call x1, Pallas kernels, shards(): pl.pallas_call(back_kernel, out_shape=pltpu.HBM(shape, F32), in_specs=[vm...  1.05 us

profile of v5, /device:TPU:232, one launch (start us, length us, event | category | flops | bytes accessed | tf_op | source)
XLA Modules:
  0.0 21.8 jit_solution(10524863698039491636)
XLA Ops:
  0.0 20.7 %implicit_sweep.1 = (f32[32,64,128]{2,1,0:T(8,128)S(1)}, f32[32,64,128]{2,1,0:T(8,128)S(1)}, f32[32,64,128]{2,1,0:T(8,128)S(1)}, f32[32,64,128]{2,1,0:T(8,128)S(1)}, f32[2,64,128]{2,1,0:T(8,128)S(1)}) custom-call(f32[32,64,128]{2,1,0:T(8,128)} %u_hbm.1, f32[32,64,128]{2,1,0:T(8,128)} %k_hbm.1, f32[64,128]{1,0:T(8,128)} %ky_hbm.1, f32[64,128]{1,0:T(8,128)} %kz_hbm.1), custom_call_target="tpu_custom_call" | custom-call | tf_op jit(solution)/shard_map/implicit_sweep/pallas_call | solution.py:358
  20.8 1.0 %back_substitution.1 = f32[32,64,128]{2,1,0:T(8,128)} custom-call(f32[32,64,128]{2,1,0:T(8,128)S(1)} %get-tuple-element.10.u, f32[32,64,128]{2,1,0:T(8,128)S(1)} %get-tuple-element.11.fl, f32[32,64,128]{2,1,0:T(8,128)S(1)} %get-tuple-element.12.fr, f32[32,64,128]{2,1,0:T(8,128)S(1)} %get-tuple-element.13.rg, f32[2,64,128]{2,1,0:T(8,128)S(1)} %get-tuple-element.14.w), custom_call_target="tpu_custom_call" | custom-call | tf_op jit(solution)/shard_map/back_substitution/pallas_call | solution.py:379

commit v6 on v5

--- a/solution.py
+++ b/solution.py
@@ -25,7 +25,7 @@
     return min(a, n - a)
 
 
-SOLVERS = (1, 4, 28, 2, 24, 29, 6, 9, 11, 12, 20, 25, 16, 15, 13, 3)
+SOLVERS = (1, 4, 28, 2, 24, 29, 6, 9, 11, 12, 20, 25, 16, 10, 13, 3)
 
 
 OFFSETS = sorted(
@@ -174,11 +174,11 @@
     send_down[pl.ds(L, 8), :] = jnp.broadcast_to(ky[pl.ds(0, 1), :], (8, 128))
     up = pltpu.make_async_remote_copy(
         src_ref=send_up, dst_ref=from_below, send_sem=halo_send_sem.at[0],
-        recv_sem=halo_recv_sem.at[0], device_id=(me, z + 1), device_id_type=MESH,
+        recv_sem=halo_recv_sem.at[0], device_id=(me, lax.rem(z + 1, NYZ)), device_id_type=MESH,
     )
     down = pltpu.make_async_remote_copy(
         src_ref=send_down, dst_ref=from_above, send_sem=halo_send_sem.at[1],
-        recv_sem=halo_recv_sem.at[1], device_id=(me, z - 1), device_id_type=MESH,
+        recv_sem=halo_recv_sem.at[1], device_id=(me, lax.rem(z + NYZ - 1, NYZ)), device_id_type=MESH,
     )
 
     @pl.when(z == 0)

time: 21.9 us -> 21.8 us (level)
  the two profiles are of different devices: /device:TPU:232 before, /device:TPU:193 now
where the time goes in v6:
time: 21.8 us; the launch traced here: 21.7 us
  Pallas kernels  21.7 us (100%)
    pallas_call x1, Pallas kernels, shards(): pl.pallas_call(sweep_kernel, out_shape=(field, field, field, field, pltpu...  20.6 us
    pallas_call x1, Pallas kernels, shards(): pl.pallas_call(back_kernel, out_shape=pltpu.HBM(shape, F32), in_specs=[vm...  1.05 us

profile of v6, /device:TPU:193, one launch (start us, length us, event | category | flops | bytes accessed | tf_op | source)
XLA Modules:
  0.0 21.7 jit_solution(11292265367639022993)
XLA Ops:
  0.0 20.6 %implicit_sweep.1 = (f32[32,64,128]{2,1,0:T(8,128)S(1)}, f32[32,64,128]{2,1,0:T(8,128)S(1)}, f32[32,64,128]{2,1,0:T(8,128)S(1)}, f32[32,64,128]{2,1,0:T(8,128)S(1)}, f32[2,64,128]{2,1,0:T(8,128)S(1)}) custom-call(f32[32,64,128]{2,1,0:T(8,128)} %u_hbm.1, f32[32,64,128]{2,1,0:T(8,128)} %k_hbm.1, f32[64,128]{1,0:T(8,128)} %ky_hbm.1, f32[64,128]{1,0:T(8,128)} %kz_hbm.1), custom_call_target="tpu_custom_call" | custom-call | tf_op jit(solution)/shard_map/implicit_sweep/pallas_call | solution.py:358
  20.7 1.0 %back_substitution.1 = f32[32,64,128]{2,1,0:T(8,128)} custom-call(f32[32,64,128]{2,1,0:T(8,128)S(1)} %get-tuple-element.10.u, f32[32,64,128]{2,1,0:T(8,128)S(1)} %get-tuple-element.11.fl, f32[32,64,128]{2,1,0:T(8,128)S(1)} %get-tuple-element.12.fr, f32[32,64,128]{2,1,0:T(8,128)S(1)} %get-tuple-element.13.rg, f32[2,64,128]{2,1,0:T(8,128)S(1)} %get-tuple-element.14.w), custom_call_target="tpu_custom_call" | custom-call | tf_op jit(solution)/shard_map/back_substitution/pallas_call | solution.py:379

commit v7 on v6

--- a/solution.py
+++ b/solution.py
@@ -329,8 +329,8 @@
     value = w[1]
     out[L - 1] = value - u[L - 1]
     stores = []
-    for low in range(L - PART, -1, -PART):
-        top = low + PART - 1
+    for low in range(L - STEP, -1, -STEP):
+        top = low + STEP - 1
         if top == L - 1:
             for i in range(top - 1, top - STEP, -1):
                 value = back(i, value)
@@ -342,8 +342,8 @@
             return value
 
         value = lax.fori_loop(0, (top + 1 - low) // STEP, step, value)
-        part = pl.ds(low, PART)
-        stores.append(pltpu.make_async_copy(out.at[part], out_hbm.at[part], store_sem.at[low // PART]))
+        part = pl.ds(low, STEP)
+        stores.append(pltpu.make_async_copy(out.at[part], out_hbm.at[part], store_sem.at[low // STEP]))
         stores[-1].start()
     for c in stores:
         c.wait()
@@ -381,7 +381,7 @@
         out_shape=pltpu.HBM(shape, F32),
         in_specs=[vmem] * 5,
         out_specs=any_space,
-        scratch_shapes=[field, pltpu.SemaphoreType.DMA((L // PART,))],
+        scratch_shapes=[field, pltpu.SemaphoreType.DMA((L // STEP,))],
         compiler_params=pltpu.CompilerParams(vmem_limit_bytes=16 * 1024 * 1024),
         name="back_substitution",
     )(*(pltpu.with_memory_space_constraint(a, pltpu.VMEM) for a in blocks))

time: 21.8 us -> 21.8 us (level)
  no operation moved by 1% of the time
where the time goes in v7:
time: 21.8 us; the launch traced here: 21.7 us
  Pallas kernels  21.7 us (100%)
    pallas_call x1, Pallas kernels, shards(): pl.pallas_call(sweep_kernel, out_shape=(field, field, field, field, pltpu...  20.6 us
    pallas_call x1, Pallas kernels, shards(): pl.pallas_call(back_kernel, out_shape=pltpu.HBM(shape, F32), in_specs=[vm...  1.05 us

profile of v7, /device:TPU:193, one launch (start us, length us, event | category | flops | bytes accessed | tf_op | source)
XLA Modules:
  0.0 21.7 jit_solution(13614486919604065970)
XLA Ops:
  0.0 20.6 %implicit_sweep.1 = (f32[32,64,128]{2,1,0:T(8,128)S(1)}, f32[32,64,128]{2,1,0:T(8,128)S(1)}, f32[32,64,128]{2,1,0:T(8,128)S(1)}, f32[32,64,128]{2,1,0:T(8,128)S(1)}, f32[2,64,128]{2,1,0:T(8,128)S(1)}) custom-call(f32[32,64,128]{2,1,0:T(8,128)} %u_hbm.1, f32[32,64,128]{2,1,0:T(8,128)} %k_hbm.1, f32[64,128]{1,0:T(8,128)} %ky_hbm.1, f32[64,128]{1,0:T(8,128)} %kz_hbm.1), custom_call_target="tpu_custom_call" | custom-call | tf_op jit(solution)/shard_map/implicit_sweep/pallas_call | solution.py:358
  20.7 1.1 %back_substitution.1 = f32[32,64,128]{2,1,0:T(8,128)} custom-call(f32[32,64,128]{2,1,0:T(8,128)S(1)} %get-tuple-element.10.u, f32[32,64,128]{2,1,0:T(8,128)S(1)} %get-tuple-element.11.fl, f32[32,64,128]{2,1,0:T(8,128)S(1)} %get-tuple-element.12.fr, f32[32,64,128]{2,1,0:T(8,128)S(1)} %get-tuple-element.13.rg, f32[2,64,128]{2,1,0:T(8,128)S(1)} %get-tuple-element.14.w), custom_call_target="tpu_custom_call" | custom-call | tf_op jit(solution)/shard_map/back_substitution/pallas_call | solution.py:379
